TPU v7x, 128 devices: a whole 4x4x4 slice. The times are simulated.
128 devices in a mesh: ia: 32 (over x_hi, y, z), ja: 4 (over x_lo, core).
Axes of the slice: x: 4 (x_hi: 2, x_lo: 2; x = x_hi * 2 + x_lo), y: 4, z: 4, core: 2. Of those that a mesh axis runs over, the one named last changes fastest.
Arguments:
- field: float32 [2, 75, 128, 4096], P(None, None, 'ja', 'ia'), may hold values from -30 to 30
- diff_i: float32 [2, 75, 128, 4096], P(None, None, 'ja', 'ia'), may hold values from 0.5 to 8
- diff_j: float32 [2, 75, 128, 4096], P(None, None, 'ja', 'ia'), may hold values from 0.5 to 8
- land_sea: int32 [75, 128, 4096], P(None, 'ja', 'ia'), may hold values 0 or 1
- partner: int32 [4096], replicated, may hold values from 0 to 4095, as said below
- vertical: float32 [2, 75, 75], replicated, may hold values from -0.5 to 2
Outputs:
- correlated: float32 [2, 75, 128, 4096], P(None, None, 'ja', 'ia')
Inputs may be any that keep to these rules, and one draw needn't show every extreme that they name: partner[i] = (c - i) mod 4096 for one column c that is the same for every i, so partner[partner[i]] = i.
All inputs are finite; a program needn't handle non-finite values. No bound on the sum of `land_sea` on one device may be relied on, other than what follows from the above.
Results may differ from a plain program's by a relative error of at most 0.000082.
Values sent between devices are 32-bit elements; how exact they have to be, the bound alone decides.
No kernel may reach another device: no remote copies, remote signals or barrier semaphores. Data moves between devices by JAX's collectives and lax.ppermute only.
A program may use at most 192 MiB of HBM per device.

v0:
```python
import jax
import jax.numpy as jnp
from jax import lax
from jax.sharding import PartitionSpec as P

ITERS = 4


diff_ceiling = 8.0


def with_halo(block, sides, width, periodic):
    for axis, dim in sides:
        count = lax.axis_size(axis)
        forward = [(i, i + 1) for i in range(count - 1)]
        if periodic:
            forward.append((count - 1, 0))
        backward = [(target, source) for source, target in forward]
        low = lax.ppermute(
            lax.slice_in_dim(block, block.shape[dim] - width, None, axis=dim), axis, forward
        )
        high = lax.ppermute(lax.slice_in_dim(block, 0, width, axis=dim), axis, backward)
        block = jnp.concatenate([low, block, high], axis=dim)
    return block


def chebyshev_steps(count):
    lowest_eig = 1.0
    highest_eig = 1.0 + 8.0 * diff_ceiling
    centre_val = 0.5 * (highest_eig + lowest_eig)
    half_width = 0.5 * (highest_eig - lowest_eig)
    plan = []
    step_size = 1.0 / centre_val
    momentum = 0.0
    plan.append((step_size, momentum))
    for turn_index in range(1, count):
        if turn_index == 1:
            momentum = 0.5 * (half_width * step_size) ** 2
        else:
            momentum = (0.5 * half_width * step_size) ** 2
        step_size = 1.0 / (centre_val - momentum / step_size)
        plan.append((step_size, momentum))
    return plan


def folded(top_rows, my_partners):
    lead_shape = top_rows.shape[:-1]
    cols_here = top_rows.shape[-1]
    level_rows = top_rows.reshape(-1, cols_here)
    full_row = lax.all_gather(level_rows, "ia", axis=1, tiled=True)
    fold_ghost = jnp.take(full_row, my_partners, axis=1)
    return fold_ghost.reshape(lead_shape + (cols_here,))


def neighbours(values, my_partners):
    rows_here = values.shape[2]
    at_top = lax.axis_index("ja") == lax.axis_size("ja") - 1
    zonal_pad = with_halo(values, (("ia", 3),), 1, True)
    merid_pad = with_halo(values, (("ja", 2),), 1, False)
    lower_row = merid_pad[:, :, 0, :]
    east_side = zonal_pad[..., 2:]
    west_side = zonal_pad[..., :-2]
    fold_ghost = folded(values[:, :, rows_here - 1, :], my_partners)
    upper_row = jnp.where(at_top, fold_ghost, merid_pad[:, :, rows_here + 1, :])
    north_side = jnp.concatenate(
        [merid_pad[:, :, 2 : rows_here + 1, :], upper_row[:, :, None, :]], axis=2
    )
    south_side = jnp.concatenate(
        [lower_row[:, :, None, :], merid_pad[:, :, 1:rows_here, :]], axis=2
    )
    return (east_side, west_side, north_side, south_side)


def body(field, diff_i, diff_j, land_sea, partner, vertical):
    num_fields, num_levels, rows_here, cols_here = field.shape
    wet_cells = land_sea.astype(jnp.float32)
    first_col = lax.axis_index("ia") * cols_here
    my_partners = lax.dynamic_slice_in_dim(partner, first_col, cols_here)
    zonal_root = jnp.sqrt(diff_i) * wet_cells[None]
    merid_root = jnp.sqrt(diff_j) * wet_cells[None]
    plan = chebyshev_steps(ITERS)
    source = field * wet_cells[None]
    stacked = jnp.concatenate([zonal_root, merid_root], axis=0)
    root_sides = neighbours(stacked, my_partners)
    zonal_east = root_sides[0][:num_fields]
    zonal_west = root_sides[1][:num_fields]
    merid_north = root_sides[2][num_fields:]
    merid_south = root_sides[3][num_fields:]
    iterate = jnp.zeros_like(source)
    residual = source
    direction = jnp.zeros_like(source)
    for turn_index in range(ITERS):
        step_size, momentum = plan[turn_index]
        direction = residual + momentum * direction
        iterate = iterate + step_size * direction
        if turn_index < ITERS - 1:
            east_side, west_side, north_side, south_side = neighbours(direction, my_partners)
            zonal_part = zonal_root * (
                zonal_east * (direction - east_side) + zonal_west * (direction - west_side)
            )
            merid_part = merid_root * (
                merid_north * (direction - north_side) + merid_south * (direction - south_side)
            )
            residual = residual - step_size * (direction + zonal_part + merid_part)
    mixed = jnp.einsum("vlm,vmji->vlji", vertical, iterate, precision=lax.Precision.HIGHEST)
    return mixed * wet_cells[None]


def solution(mesh):
    placed = (
        P(None, None, "ja", "ia"),
        P(None, None, "ja", "ia"),
        P(None, None, "ja", "ia"),
        P(None, "ja", "ia"),
        P(),
        P(),
    )
    return jax.shard_map(
        body, mesh=mesh, in_specs=placed, out_specs=P(None, None, "ja", "ia"), check_vma=False
    )
```

profile of v0, /device:TPU:3, one launch (start us, length us, event | category | flops | bytes accessed | tf_op | source)
XLA Modules:
  0.0 446.1 jit_solution(3380925370537959386)
XLA Ops:
  9.4 9.0 %fusion.60 = (f32[2,75,32,128]{3,1,2,0:T(8,128)}, f32[2,75,32,128]{3,1,2,0:T(8,128)}, f32[2,75,32,128]{3,1,2,0:T(8,128)S(1)}) fusion(f32[2,75,32,128]{3,2,1,0:T(8,128)S(1)} %copy-done.2, f32[75,32,128]{2,0,1:T(8,128)S(1)} %copy.39, f32[2,75,32,128]{3,2,1,0:T(8,128)S(1)} %copy-done.3, f32[2,75,32,128]{3,2,1,0:T(8,128)} %param.8), kind=kLoop, calls=%fused_computation.92 | loop fusion | flops 1843200 | bytes 15974400 | tf_op jit(solution)/shard_map/mul | solution.py:79
  24.7 3.1 fusion.93
  34.8 6.2 %collective-permute-start.1 = (f32[2,75,32,1]{1,2,3,0:T(8,128)S(1)}, f32[2,75,32,1]{1,2,3,0:T(8,128)S(1)}, u32[]{:S(2)}, u32[]{:S(2)}) collective-permute-start(f32[2,75,32,1]{1,2,3,0:T(8,128)S(1)} %copy.45), channel_id=1, source_target_pairs={{4,0},{8,4},{12,8},{16,12},{20,16},{24,20},{28,24},{32,28},{36,32}... | collective-permute-start | bytes 57608 | tf_op jit(solution)/shard_map/ppermute | solution.py:22
  40.9 7.4 %fusion = (f32[4,75,32,1]{3,1,2,0:T(8,128)}, f32[4,75,32,1]{3,1,2,0:T(8,128)}) fusion(f32[2,75,32,128]{3,1,2,0:T(8,128)} %get-tuple-element.32, f32[2,75,32,128]{3,1,2,0:T(8,128)} %get-tuple-element.33), kind=kLoop, calls=%fused_computation.14 | loop fusion | flops 19200 | bytes 4992000 | tf_op jit(solution)/shard_map/concatenate | solution.py:83
  48.4 3.5 copy.47
  51.9 3.5 copy.43
  55.4 7.3 %collective-permute-start = (f32[4,75,32,1]{1,2,3,0:T(8,128)S(1)}, f32[4,75,32,1]{1,2,3,0:T(8,128)S(1)}, u32[]{:S(2)}, u32[]{:S(2)}) collective-permute-start(f32[4,75,32,1]{1,2,3,0:T(8,128)S(1)} %copy.43), channel_id=1, source_target_pairs={{4,0},{8,4},{12,8},{16,12},{20,16},{24,20},{28,24},{32,28},{36,32}... | collective-permute-start | bytes 115208 | tf_op jit(solution)/shard_map/ppermute | solution.py:22
  63.4 5.3 %fusion.2 = f32[4,75,31,128]{3,1,2,0:T(8,128)} fusion(f32[2,75,32,128]{3,1,2,0:T(8,128)} %get-tuple-element.32, f32[2,75,32,128]{3,1,2,0:T(8,128)} %get-tuple-element.33), kind=kLoop, calls=%fused_computation.16 | loop fusion | flops 1190400 | bytes 9676800 | tf_op jit(solution)/shard_map/concatenate | solution.py:83
  75.3 5.3 %collective-permute-start.5 = (f32[2,75,1,128]{3,1,2,0:T(8,128)S(1)}, f32[2,75,1,128]{3,1,2,0:T(8,128)}, u32[]{:S(2)}, u32[]{:S(2)}) collective-permute-start(f32[2,75,1,128]{3,1,2,0:T(8,128)S(1)} %get-tuple-element.30), channel_id=1, source_target_pairs={{1,0},{2,1},{3,2},{5,4},{6,5},{7,6},{9,8},{10,9},{11,10},{13,12},{... | collective-permute-start | bytes 230408 | tf_op jit(solution)/shard_map/ppermute | solution.py:22
  83.0 3.7 collective-permute-start.4
  86.7 3.3 copy.44
  89.9 3.3 copy.48
  93.2 12.4 %all-gather.7.cloned.1.call-done = f32[150,4096]{0,1:T(8,128)} async-done(((f32[150,128]{0,1:T(8,128)}), f32[150,4096]{0,1:T(8,128)}) %all-gather.7.cloned.1.call-update) | async-done | bytes 2457616 | tf_op jit(solution)/shard_map/all_gather | solution.py:50
  105.6 2.9 gather_fusion.1
  108.9 90.4 %all-gather.5.cloned.1.call-done = f32[300,4096]{0,1:T(8,128)} async-done(((f32[300,128]{0,1:T(8,128)}), f32[300,4096]{0,1:T(8,128)}) %all-gather.5.cloned.1.call-update) | async-done | bytes 4915216 | tf_op jit(solution)/shard_map/all_gather | solution.py:50
  199.3 4.3 gather_fusion
  206.5 15.5 %multiply_add_fusion.1 = (f32[2,75,32,128]{3,1,2,0:T(8,128)}, f32[2,75,32,128]{3,1,2,0:T(8,128)}) fusion(f32[2,75,32,128]{3,1,2,0:T(8,128)S(1)} %get-tuple-element.34, f32[2,75,32,128]{3,1,2,0:T(8,128)} %get-tuple-element.33, f32[2,75,31,128]{3,1,2,0:T(8,128)} %get-tuple-element.29, f32[2,75,1,128]{3,1,2,0:T(8,128)} %collective-permute-done.7, ...), kind=kLoop, calls=%fused_computation.100 | loop fusion | flops 17817600 | bytes 22387200 | tf_op jit(solution)/shard_map/add | solution.py:94
  225.7 5.6 %fusion.90 = (f32[2,75,32,1]{3,1,2,0:T(8,128)}, f32[2,75,32,1]{3,1,2,0:T(8,128)}) fusion(f32[2,75,32,128]{3,1,2,0:T(8,128)} %get-tuple-element.6), kind=kLoop, calls=%fused_computation.131 | loop fusion | bytes 76800 | tf_op jit(solution)/shard_map/slice | solution.py:22
  237.9 6.0 %collective-permute-start.8 = (f32[2,75,32,1]{1,2,3,0:T(8,128)S(1)}, f32[2,75,32,1]{1,2,3,0:T(8,128)S(1)}, u32[]{:S(2)}, u32[]{:S(2)}) collective-permute-start(f32[2,75,32,1]{1,2,3,0:T(8,128)S(1)} %copy.57), channel_id=1, source_target_pairs={{4,0},{8,4},{12,8},{16,12},{20,16},{24,20},{28,24},{32,28},{36,32}... | collective-permute-start | bytes 57608 | tf_op jit(solution)/shard_map/ppermute | solution.py:22
  243.8 5.3 %fusion.91 = (f32[2,75,31,128]{3,1,2,0:T(8,128)}, f32[2,75,31,128]{3,1,2,0:T(8,128)}) fusion(f32[2,75,32,128]{3,1,2,0:T(8,128)} %get-tuple-element.6), kind=kLoop, calls=%fused_computation.132 | loop fusion | bytes 9523200 | tf_op jit(solution)/shard_map/slice | solution.py:66
  249.2 4.8 %collective-permute-start.10 = (f32[2,75,1,128]{3,1,2,0:T(8,128)}, f32[2,75,1,128]{3,1,2,0:T(8,128)}, u32[]{:S(2)}, u32[]{:S(2)}) collective-permute-start(f32[2,75,1,128]{3,1,2,0:T(8,128)} %get-tuple-element.24), channel_id=1, source_target_pairs={{1,0},{2,1},{3,2},{5,4},{6,5},{7,6},{9,8},{10,9},{11,10},{13,12},{... | collective-permute-start | bytes 230408 | tf_op jit(solution)/shard_map/ppermute | solution.py:22
  258.8 44.4 %all-gather.9.cloned.1.call-done = f32[150,4096]{0,1:T(8,128)} async-done(((f32[150,128]{0,1:T(8,128)}), f32[150,4096]{0,1:T(8,128)}) %all-gather.9.cloned.1.call-update) | async-done | bytes 2457616 | tf_op jit(solution)/shard_map/all_gather | solution.py:50
  303.1 2.9 gather_fusion.2
  306.4 17.6 %multiply_add_fusion = f32[2,75,32,128]{3,1,2,0:T(8,128)} fusion(f32[2,75,32,128]{3,1,2,0:T(8,128)} %get-tuple-element.7, f32[2,75,32,128]{3,1,2,0:T(8,128)S(1)} %get-tuple-element.34, f32[2,75,32,128]{3,1,2,0:T(8,128)} %get-tuple-element.33, f32[2,75,32,128]{3,1,2,0:T(8,128)} %get-tuple-element.6, f32[2,75,31,128]{3,1,2,0:T(8,128)} %get-tuple-element.23, ...), kind=kLoop, calls=%fused_computation.97 | loop fusion | flops 19046400 | bytes 24844800 | tf_op jit(solution)/shard_map/add | solution.py:94
  327.7 5.6 %fusion.89 = (f32[2,75,32,1]{3,1,2,0:T(8,128)}, f32[2,75,32,1]{3,1,2,0:T(8,128)}) fusion(f32[2,75,32,128]{3,1,2,0:T(8,128)} %multiply_add_fusion), kind=kLoop, calls=%fused_computation.130 | loop fusion | bytes 76800 | tf_op jit(solution)/shard_map/slice | solution.py:22
  339.8 6.0 %collective-permute-start.12 = (f32[2,75,32,1]{1,2,3,0:T(8,128)S(1)}, f32[2,75,32,1]{1,2,3,0:T(8,128)S(1)}, u32[]{:S(2)}, u32[]{:S(2)}) collective-permute-start(f32[2,75,32,1]{1,2,3,0:T(8,128)S(1)} %copy.64), channel_id=1, source_target_pairs={{4,0},{8,4},{12,8},{16,12},{20,16},{24,20},{28,24},{32,28},{36,32}... | collective-permute-start | bytes 57608 | tf_op jit(solution)/shard_map/ppermute | solution.py:22
  345.8 5.2 %fusion.87 = (f32[2,75,31,128]{3,1,2,0:T(8,128)}, f32[2,75,31,128]{3,1,2,0:T(8,128)}) fusion(f32[2,75,32,128]{3,1,2,0:T(8,128)} %multiply_add_fusion), kind=kLoop, calls=%fused_computation.128 | loop fusion | bytes 9523200 | tf_op jit(solution)/shard_map/slice | solution.py:69
  351.0 5.8 %collective-permute-start.14 = (f32[2,75,1,128]{3,1,2,0:T(8,128)}, f32[2,75,1,128]{3,1,2,0:T(8,128)}, u32[]{:S(2)}, u32[]{:S(2)}) collective-permute-start(f32[2,75,1,128]{3,1,2,0:T(8,128)} %get-tuple-element.16), channel_id=1, source_target_pairs={{1,0},{2,1},{3,2},{5,4},{6,5},{7,6},{9,8},{10,9},{11,10},{13,12},{... | collective-permute-start | bytes 230408 | tf_op jit(solution)/shard_map/ppermute | solution.py:22
  361.8 45.3 %all-gather.11.cloned.1.call-done = f32[150,4096]{0,1:T(8,128)} async-done(((f32[150,128]{0,1:T(8,128)}), f32[150,4096]{0,1:T(8,128)}) %all-gather.11.cloned.1.call-update) | async-done | bytes 2457616 | tf_op jit(solution)/shard_map/all_gather | solution.py:50
  407.0 2.9 gather_fusion.3
  411.9 23.8 %bitcast_multiply_fusion = f32[2,75,32,128]{3,1,2,0:T(8,128)} fusion(f32[2,75,32,128]{3,1,2,0:T(8,128)} %multiply_add_fusion, f32[2,75,32,128]{3,1,2,0:T(8,128)} %get-tuple-element.32, f32[2,75,32,1]{3,1,2,0:T(8,128)} %copy.67, f32[2,75,32,1]{3,1,2,0:T(8,128)} %copy.65, f32[2,75,32,128]{3,1,2,0:T(8,128)} %get-tuple-element.33, ...), kind=kOutput, calls=%fused_computation.88 | convolution fusion | flops 589209600 | bytes 33529800 | tf_op jit(solution)/shard_map/vlm,vmji->vlji/dot_general | solution.py:105
  435.7 3.9 copy.72
  (84 shorter events, 61.2 us)
Async XLA Ops:
  6.5 405.3 %copy-start = (f32[2,75,75]{2,0,1:T(2,128)S(1)}, f32[2,75,75]{2,0,1:T(2,128)}, u32[]{:S(2)}) copy-start(f32[2,75,75]{2,0,1:T(2,128)} %param.13) | copy-start | bytes 135004
  6.5 99.1 %all-gather.7.cloned.1.call-start = ((), (), s32[]{:S(2)}) async-start(), calls=%async_computation.1 | async-start | bytes 4325376 | tf_op jit(solution)/shard_map/all_gather | solution.py:50
  6.5 2.3 copy-start.2
  6.5 2.8 copy-start.3
  9.4 9.0 %copy-start.1 = (f32[75,32,128]{2,0,1:T(8,128)}, f32[75,32,128]{2,0,1:T(8,128)S(1)}, u32[]{:S(2)}) copy-start(f32[75,32,128]{2,0,1:T(8,128)S(1)} %copy.39) | copy-start | bytes 3686404
  20.7 178.5 %all-gather.5.cloned.1.call-start = ((), (), s32[]{:S(2)}) async-start(), calls=%async_computation | async-start | bytes 6488064 | tf_op jit(solution)/shard_map/all_gather | solution.py:50
  23.4 279.7 %all-gather.9.cloned.1.call-start = ((), (), s32[]{:S(2)}) async-start(), calls=%async_computation.2 | async-start | bytes 4325376 | tf_op jit(solution)/shard_map/all_gather | solution.py:50
  23.4 183.0 %collective-permute-start.7 = (f32[2,75,1,128]{3,1,2,0:T(8,128)}, f32[2,75,1,128]{3,1,2,0:T(8,128)}, u32[]{:S(2)}, u32[]{:S(2)}) collective-permute-start(f32[2,75,1,128]{3,1,2,0:T(8,128)} %get-tuple-element.31), channel_id=1, source_target_pairs={{0,1},{1,2},{2,3},{4,5},{5,6},{6,7},{8,9},{9,10},{10,11},{12,13},{... | collective-permute-start | bytes 230408 | tf_op jit(solution)/shard_map/ppermute | solution.py:19
  30.5 44.8 %collective-permute-start.3 = (f32[2,75,32,1]{1,2,3,0:T(8,128)S(1)}, f32[2,75,32,1]{1,2,3,0:T(8,128)S(1)}, u32[]{:S(2)}, u32[]{:S(2)}) collective-permute-start(f32[2,75,32,1]{1,2,3,0:T(8,128)S(1)} %copy.49), channel_id=1, source_target_pairs={{0,4},{4,8},{8,12},{12,16},{16,20},{20,24},{24,28},{28,32},{32,36}... | collective-permute-start | bytes 57608 | tf_op jit(solution)/shard_map/ppermute | solution.py:19
  34.8 36.6 %collective-permute-start.1 = (f32[2,75,32,1]{1,2,3,0:T(8,128)S(1)}, f32[2,75,32,1]{1,2,3,0:T(8,128)S(1)}, u32[]{:S(2)}, u32[]{:S(2)}) collective-permute-start(f32[2,75,32,1]{1,2,3,0:T(8,128)S(1)} %copy.45), channel_id=1, source_target_pairs={{4,0},{8,4},{12,8},{16,12},{20,16},{24,20},{28,24},{32,28},{36,32}... | collective-permute-start | bytes 57608 | tf_op jit(solution)/shard_map/ppermute | solution.py:22
  51.8 38.1 %collective-permute-start.2 = (f32[4,75,32,1]{1,2,3,0:T(8,128)S(1)}, f32[4,75,32,1]{1,2,3,0:T(8,128)S(1)}, u32[]{:S(2)}, u32[]{:S(2)}) collective-permute-start(f32[4,75,32,1]{1,2,3,0:T(8,128)S(1)} %copy.47), channel_id=1, source_target_pairs={{0,4},{4,8},{8,12},{12,16},{16,20},{20,24},{24,28},{28,32},{32,36}... | collective-permute-start | bytes 115208 | tf_op jit(solution)/shard_map/ppermute | solution.py:19
  55.4 27.6 %collective-permute-start = (f32[4,75,32,1]{1,2,3,0:T(8,128)S(1)}, f32[4,75,32,1]{1,2,3,0:T(8,128)S(1)}, u32[]{:S(2)}, u32[]{:S(2)}) collective-permute-start(f32[4,75,32,1]{1,2,3,0:T(8,128)S(1)} %copy.43), channel_id=1, source_target_pairs={{4,0},{8,4},{12,8},{16,12},{20,16},{24,20},{28,24},{32,28},{36,32}... | collective-permute-start | bytes 115208 | tf_op jit(solution)/shard_map/ppermute | solution.py:22
  71.4 135.1 %collective-permute-start.6 = (f32[4,75,1,128]{3,1,2,0:T(8,128)S(1)}, f32[4,75,1,128]{3,1,2,0:T(8,128)S(1)}, u32[]{:S(2)}, u32[]{:S(2)}) collective-permute-start(f32[4,75,1,128]{3,1,2,0:T(8,128)S(1)} %get-tuple-element.13), channel_id=1, source_target_pairs={{0,1},{1,2},{2,3},{4,5},{5,6},{6,7},{8,9},{9,10},{10,11},{12,13},{... | collective-permute-start | bytes 460808 | tf_op jit(solution)/shard_map/ppermute | solution.py:19
  75.3 33.6 %collective-permute-start.5 = (f32[2,75,1,128]{3,1,2,0:T(8,128)S(1)}, f32[2,75,1,128]{3,1,2,0:T(8,128)}, u32[]{:S(2)}, u32[]{:S(2)}) collective-permute-start(f32[2,75,1,128]{3,1,2,0:T(8,128)S(1)} %get-tuple-element.30), channel_id=1, source_target_pairs={{1,0},{2,1},{3,2},{5,4},{6,5},{7,6},{9,8},{10,9},{11,10},{13,12},{... | collective-permute-start | bytes 230408 | tf_op jit(solution)/shard_map/ppermute | solution.py:22
  83.0 122.5 %collective-permute-start.4 = (f32[4,75,1,128]{3,1,2,0:T(8,128)}, f32[4,75,1,128]{3,1,2,0:T(8,128)}, u32[]{:S(2)}, u32[]{:S(2)}) collective-permute-start(f32[4,75,1,128]{3,1,2,0:T(8,128)} %get-tuple-element.12), channel_id=1, source_target_pairs={{1,0},{2,1},{3,2},{5,4},{6,5},{7,6},{9,8},{10,9},{11,10},{13,12},{... | collective-permute-start | bytes 460808 | tf_op jit(solution)/shard_map/ppermute | solution.py:22
  224.4 182.7 %all-gather.11.cloned.1.call-start = ((), (), s32[]{:S(2)}) async-start(), calls=%async_computation.3 | async-start | bytes 4325376 | tf_op jit(solution)/shard_map/all_gather | solution.py:50
  224.4 82.0 %collective-permute-start.11 = (f32[2,75,1,128]{3,1,2,0:T(8,128)S(1)}, f32[2,75,1,128]{3,1,2,0:T(8,128)S(1)}, u32[]{:S(2)}, u32[]{:S(2)}) collective-permute-start(f32[2,75,1,128]{3,1,2,0:T(8,128)S(1)} %get-tuple-element.25), channel_id=1, source_target_pairs={{0,1},{1,2},{2,3},{4,5},{5,6},{6,7},{8,9},{9,10},{10,11},{12,13},{... | collective-permute-start | bytes 230408 | tf_op jit(solution)/shard_map/ppermute | solution.py:19
  236.6 19.8 %collective-permute-start.9 = (f32[2,75,32,1]{1,2,3,0:T(8,128)S(1)}, f32[2,75,32,1]{1,2,3,0:T(8,128)S(1)}, u32[]{:S(2)}, u32[]{:S(2)}) collective-permute-start(f32[2,75,32,1]{1,2,3,0:T(8,128)S(1)} %copy.59), channel_id=1, source_target_pairs={{0,4},{4,8},{8,12},{12,16},{16,20},{20,24},{24,28},{28,32},{32,36}... | collective-permute-start | bytes 57608 | tf_op jit(solution)/shard_map/ppermute | solution.py:19
  237.9 16.1 %collective-permute-start.8 = (f32[2,75,32,1]{1,2,3,0:T(8,128)S(1)}, f32[2,75,32,1]{1,2,3,0:T(8,128)S(1)}, u32[]{:S(2)}, u32[]{:S(2)}) collective-permute-start(f32[2,75,32,1]{1,2,3,0:T(8,128)S(1)} %copy.57), channel_id=1, source_target_pairs={{4,0},{8,4},{12,8},{16,12},{20,16},{24,20},{28,24},{32,28},{36,32}... | collective-permute-start | bytes 57608 | tf_op jit(solution)/shard_map/ppermute | solution.py:22
  249.2 57.2 %collective-permute-start.10 = (f32[2,75,1,128]{3,1,2,0:T(8,128)}, f32[2,75,1,128]{3,1,2,0:T(8,128)}, u32[]{:S(2)}, u32[]{:S(2)}) collective-permute-start(f32[2,75,1,128]{3,1,2,0:T(8,128)} %get-tuple-element.24), channel_id=1, source_target_pairs={{1,0},{2,1},{3,2},{5,4},{6,5},{7,6},{9,8},{10,9},{11,10},{13,12},{... | collective-permute-start | bytes 230408 | tf_op jit(solution)/shard_map/ppermute | solution.py:22
  326.4 85.4 %collective-permute-start.15 = (f32[2,75,1,128]{3,1,2,0:T(8,128)S(1)}, f32[2,75,1,128]{3,1,2,0:T(8,128)}, u32[]{:S(2)}, u32[]{:S(2)}) collective-permute-start(f32[2,75,1,128]{3,1,2,0:T(8,128)S(1)} %get-tuple-element.17), channel_id=1, source_target_pairs={{0,1},{1,2},{2,3},{4,5},{5,6},{6,7},{8,9},{9,10},{10,11},{12,13},{... | collective-permute-start | bytes 230408 | tf_op jit(solution)/shard_map/ppermute | solution.py:19
  338.6 20.7 %collective-permute-start.13 = (f32[2,75,32,1]{1,2,3,0:T(8,128)S(1)}, f32[2,75,32,1]{1,2,3,0:T(8,128)S(1)}, u32[]{:S(2)}, u32[]{:S(2)}) collective-permute-start(f32[2,75,32,1]{1,2,3,0:T(8,128)S(1)} %copy.66), channel_id=1, source_target_pairs={{0,4},{4,8},{8,12},{12,16},{16,20},{20,24},{24,28},{28,32},{32,36}... | collective-permute-start | bytes 57608 | tf_op jit(solution)/shard_map/ppermute | solution.py:19
  339.8 17.0 %collective-permute-start.12 = (f32[2,75,32,1]{1,2,3,0:T(8,128)S(1)}, f32[2,75,32,1]{1,2,3,0:T(8,128)S(1)}, u32[]{:S(2)}, u32[]{:S(2)}) collective-permute-start(f32[2,75,32,1]{1,2,3,0:T(8,128)S(1)} %copy.64), channel_id=1, source_target_pairs={{4,0},{8,4},{12,8},{16,12},{20,16},{24,20},{28,24},{32,28},{36,32}... | collective-permute-start | bytes 57608 | tf_op jit(solution)/shard_map/ppermute | solution.py:22
  351.0 59.9 %collective-permute-start.14 = (f32[2,75,1,128]{3,1,2,0:T(8,128)}, f32[2,75,1,128]{3,1,2,0:T(8,128)}, u32[]{:S(2)}, u32[]{:S(2)}) collective-permute-start(f32[2,75,1,128]{3,1,2,0:T(8,128)} %get-tuple-element.16), channel_id=1, source_target_pairs={{1,0},{2,1},{3,2},{5,4},{6,5},{7,6},{9,8},{10,9},{11,10},{13,12},{... | collective-permute-start | bytes 230408 | tf_op jit(solution)/shard_map/ppermute | solution.py:22
Sparse Core Ops, SparseCore 0:
  20.9 84.6 all-gather.6
  108.6 90.6 all-gather.4
  224.5 78.5 all-gather.8
  326.6 80.4 all-gather.10
where the time goes:
time: 449 us; the launch traced here: 446 us
  waiting for transfers between devices  193 us (43%)
  local copies, waits for them, and re-layouts  100 us (22%)
  other arithmetic  61.2 us (14%)
  starting transfers between devices  54.8 us (12%)
  matrix products  23.8 us (5%)
  between operations  13.4 us (3%)
    all_gather x4, waiting for transfers between devices, folded(): full_row = lax.all_gather(level_rows, 'ia', axis=1, tiled=True)  192 us
    ppermute x8, starting transfers between devices, with_halo(): lax.ppermute(lax.slice_in_dim(block, 0, width, axis=dim), axis, backward)  45 us
    add x2, other arithmetic, body(): direction = residual + momentum * direction  33.2 us
    slice x10, local copies, waits for them, and re-layouts, with_halo(): lax.slice_in_dim(block, 0, width, axis=dim)  29.4 us
    dot_general x1, matrix products, body(): jnp.einsum('vlm,vmji->vlji', vertical, iterate, precision=lax.Precision.H...  23.8 us
    gather x6, local copies, waits for them, and re-layouts, folded(): fold_ghost = jnp.take(full_row, my_partners, axis=1)  15 us
    concatenate x3, other arithmetic, body(): stacked = jnp.concatenate([zonal_root, merid_root], axis=0)  14.5 us
    slice x4, local copies, waits for them, and re-layouts, with_halo(): lax.slice_in_dim(block, block.shape[dim] - width, None, axis=dim)  11.3 us
  transfers between devices with their start and end apart: 20, of which 4 were waited for; matrix products, arithmetic and copies ran while one was open for 24% of the time, Pallas kernels for 0%

commit v1 on v0

v1 whole, which is shorter than its diff:
```python
import functools
import numpy as np
import jax
import jax.numpy as jnp
from jax import lax
from jax.experimental import pallas as pl
from jax.experimental.pallas import tpu as pltpu
from jax.sharding import PartitionSpec as P

ITERS = 4
diff_ceiling = 8.0
V, L, R, C = 2, 75, 32, 128
TILES = 10
SLOTS = 8 * TILES
DEPTH = V * SLOTS
CENTRE, HALF = 33.0, 32.0
ROOT_SCALE = 32.0**-0.5


def chebyshev_steps(count):
    lowest_eig = 1.0
    highest_eig = 1.0 + 8.0 * diff_ceiling
    centre_val = 0.5 * (highest_eig + lowest_eig)
    half_width = 0.5 * (highest_eig - lowest_eig)
    plan = []
    step_size = 1.0 / centre_val
    momentum = 0.0
    plan.append((step_size, momentum))
    for turn_index in range(1, count):
        if turn_index == 1:
            momentum = 0.5 * (half_width * step_size) ** 2
        else:
            momentum = (0.5 * half_width * step_size) ** 2
        step_size = 1.0 / (centre_val - momentum / step_size)
        plan.append((step_size, momentum))
    return plan


def polynomial():
    poly = np.polynomial.polynomial
    operator = np.array([CENTRE, HALF])
    iterate = np.zeros(1)
    residual = np.ones(1)
    direction = np.zeros(1)
    for turn_index, (step_size, momentum) in enumerate(chebyshev_steps(ITERS)):
        direction = poly.polyadd(residual, momentum * direction)
        iterate = poly.polyadd(iterate, step_size * direction)
        if turn_index < ITERS - 1:
            residual = poly.polysub(residual, step_size * poly.polymul(operator, direction))
    return [float(c) for c in iterate]


POLY = polynomial()
LEAD = POLY[3]
B2, B1, B0 = POLY[2] / LEAD, POLY[1] / LEAD, POLY[0] / LEAD

GHOST = [(0, 1), (0, 2), (0, 3), (1, 1), (1, 2), (2, 1), (2, 2), (2, 3)]
PLANES = 5


def place(r):
    return divmod(r + 3, PLANES)


def lanes(rows=8):
    return lax.broadcasted_iota(jnp.int32, (rows, C), 1)


def roll(x, by):
    if isinstance(by, int):
        by = by % C
        return pltpu.roll(x, by, 1) if by else x
    return pltpu.roll(x, by & (C - 1), 1)


def slot_of(lane):
    return ((lane + 8) >> 4) & 7


def parities():
    return (lax.axis_index("ia") & 1) == 1, (lax.axis_index("ja") & 1) == 1


def start_rows(raw, kept, sems, spans):
    field, diff_i, diff_j, land = raw
    f, di, dj, ls = kept
    for v in range(V):
        at = pl.ds(v * SLOTS, L)
        for low, count in spans:

            def row(r, carry):
                pltpu.make_async_copy(field.at[v, :, r], f.at[r, at], sems.at[v]).start()
                pltpu.make_async_copy(diff_i.at[v, :, r], di.at[r, at], sems.at[2 + v]).start()
                pltpu.make_async_copy(diff_j.at[v, :, r], dj.at[r, at], sems.at[4 + v]).start()
                return carry

            lax.fori_loop(low, low + count, row, 0)


def start_land(land, ls, sem, spans):
    for low, count in spans:

        def row(r, carry):
            pltpu.make_async_copy(land.at[:, r], ls.at[r, pl.ds(0, L)], sem).start()
            return carry

        lax.fori_loop(low, low + count, row, 0)


def wait_for(ref, sem):
    pltpu.make_async_copy(ref, ref, sem).wait()


def wait_rows(kept, sems, v, count):
    for j in range(3):
        wait_for(kept[j].at[pl.ds(0, count), pl.ds(v * SLOTS, L)], sems.at[2 * j + v])


def root(x):
    return x * lax.rsqrt(x)


def cell(kept, t, k, r):
    f, di, dj, ls = kept
    at = pl.ds(pl.multiple_of(8 * t, 8), 8)
    wet = ls[r, pl.ds(pl.multiple_of(8 * k, 8), 8), :].astype(jnp.float32)
    scaled = wet * ROOT_SCALE
    return f[r, at, :] * wet, root(di[r, at, :]) * scaled, root(dj[r, at, :]) * scaled


RAW_SCRATCH = [
    pltpu.VMEM((R, DEPTH, C), jnp.float32),
    pltpu.VMEM((R, DEPTH, C), jnp.float32),
    pltpu.VMEM((R, DEPTH, C), jnp.float32),
    pltpu.VMEM((R, SLOTS, C), jnp.int32),
    pltpu.SemaphoreType.DMA((7,)),
]
ALL_ROWS = [(0, R)]


def tiles(kept, sems, count, tile):
    def body(t, carry):
        for v in range(V):

            @pl.when(t == v * TILES)
            def _():
                wait_rows(kept, sems, v, count)

        tile(t, lax.rem(t, TILES))
        return carry

    lax.fori_loop(0, DEPTH // 8, body, 0)


EDGE = 6
EDGE_ROWS = [(0, EDGE), (R - EDGE, EDGE)]
OUTER_ROWS = [(0, 3), (R - 3, 3)]


def wait_land(ls, sem, count):
    wait_for(ls.at[pl.ds(0, count), pl.ds(0, L)], sem)


def rows_kernel(field, diff_i, diff_j, land, send_a, send_b, send_x, f, di, dj, ls, sems):
    _, j_odd = parities()
    kept = (f, di, dj, ls)
    start_land(land, ls, sems.at[6], OUTER_ROWS)
    start_rows((field, diff_i, diff_j, land), kept, sems, OUTER_ROWS)
    slot = slot_of(lanes())
    wait_land(ls, sems.at[6], 6)

    def tile(t, k):
        rows = pl.ds(pl.multiple_of(8 * t, 8), 8)
        edge = {r: cell(kept, t, k, r) for r in (0, 1, 2, R - 3, R - 2, R - 1)}
        third = jnp.zeros((8, C), jnp.float32)
        for g, (a, far) in enumerate(GHOST):
            top, bottom = edge[R - far][a], edge[far - 1][a]
            send_a[g, rows, :] = jnp.where(j_odd, bottom, top)
            send_b[g, rows, :] = jnp.where(j_odd, top, bottom)
            third = jnp.where(slot == g, roll(top, 16 * g), third)
        send_x[rows, :] = third

    tiles(kept, sems, 6, tile)


def columns_kernel(
    field, diff_i, diff_j, land, columns_e, columns_o, strips, f, di, dj, ls, sems
):
    i_odd, _ = parities()
    kept = (f, di, dj, ls)
    start_land(land, ls, sems.at[6], ALL_ROWS)
    start_rows((field, diff_i, diff_j, land), kept, sems, ALL_ROWS)
    lane = lanes()
    slot = slot_of(lane)
    in_slot = lane & 15
    wait_land(ls, sems.at[6], R)

    def tile(t, k):
        rows = pl.ds(pl.multiple_of(8 * t, 8), 8)
        packed = [[jnp.zeros((8, C), jnp.float32) for _ in range(PLANES)] for _ in range(3)]
        for r in range(R):
            values = cell(kept, t, k, r)
            index, p = place(r)
            for a in range(3):
                packed[a][p] = jnp.where(slot == index, roll(values[a], 16 * index), packed[a][p])
        for a in range(3):
            left, right = packed[a][0], packed[a][0]
            for p in range(PLANES):
                strips[a, p, rows, :] = packed[a][p]
                if p:
                    left = jnp.where(in_slot >= 3 * p, roll(packed[a][p], 3 * p), left)
                    right = jnp.where(in_slot < 16 - 3 * p, roll(packed[a][p], -3 * p), right)
            columns_e[a, rows, :] = jnp.where(i_odd, left, right)
            columns_o[a, rows, :] = jnp.where(i_odd, right, left)

    tiles(kept, sems, R, tile)


WIDE = 32


def ghost_kernel(columns_e, columns_o, recv_a, recv_b, send_e, send_o):
    i_odd, j_odd = parities()
    lane = lanes(WIDE)

    def tile(t, carry):
        rows = pl.ds(pl.multiple_of(WIDE * t, 8), WIDE)
        for a in range(3):
            got_e, got_o = columns_e[a, rows, :], columns_o[a, rows, :]
            left = jnp.where(i_odd, got_e, got_o)
            right = jnp.where(i_odd, got_o, got_e)
            for g, (b, far) in enumerate(GHOST):
                if a != b:
                    continue
                one, two = recv_a[g, rows, :], recv_b[g, rows, :]
                for r, ghost in ((-far, jnp.where(j_odd, one, two)), (R - 1 + far, jnp.where(j_odd, two, one))):
                    at, p = place(r)
                    by = (16 * at + 3 * p) % C
                    here = (lane >= by) & (lane < by + 3)
                    left = jnp.where(here, roll(ghost, by), left)
                    by = (16 * at - 3 - 3 * p) % C
                    here = (lane >= by) & (lane < by + 3)
                    right = jnp.where(here, roll(ghost, by + 3), right)
            send_e[a, rows, :] = jnp.where(i_odd, left, right)
            send_o[a, rows, :] = jnp.where(i_odd, right, left)
        return carry

    lax.fori_loop(0, DEPTH // WIDE, tile, 0)


def zonal(u, edge):
    flux = edge * (u - roll(u, -1))
    return flux - roll(flux, 1)


def stream(low_row, high_row, data, emit, not_last):
    src, root_j, edge, vert, one, two = {}, {}, {}, {}, {}, {}
    n1, n2, n3 = {}, {}, {}
    lo, hi = low_row - 3, high_row + 2
    for r in range(lo, hi + 1):
        src[r], z, root_j[r] = data(r)
        if z is not None:
            edge[r] = z * not_last * roll(z, -1)
        if r == lo:
            continue
        p = r - 1
        vert[p] = root_j[p] * root_j[r]
        n1[p] = vert[p] * (src[p] - src[r])
        if p == lo:
            continue
        one[p] = (B2 - 1.0) * src[p] + zonal(src[p], edge[p]) + n1[p] - n1[p - 1]
        if p == lo + 1:
            continue
        q = p - 1
        n2[q] = vert[q] * (one[q] - one[p])
        if q == lo + 1:
            continue
        two[q] = B1 * src[q] - one[q] + zonal(one[q], edge[q]) + n2[q] - n2[q - 1]
        if q == lo + 2:
            continue
        t = q - 1
        n3[t] = vert[t] * (two[t] - two[q])
        if t == lo + 2:
            continue
        emit(t, B0 * src[t] - two[t] + zonal(two[t], edge[t]) + n3[t] - n3[t - 1])


def strip_rows(src, z, m):
    after = lambda x: [x[p + 1] if p + 1 < PLANES else roll(x[0], -16) for p in range(PLANES)]
    before = lambda x: [x[p - 1] if p else roll(x[PLANES - 1], 16) for p in range(PLANES)]
    edge = [x * roll(x, -1) for x in z]
    vert = [x * y for x, y in zip(m, after(m))]

    def apply(u, base):
        flux = [c * (x - y) for c, x, y in zip(vert, u, after(u))]
        return [
            b + zonal(x, e) + f - g
            for b, x, e, f, g in zip(base, u, edge, flux, before(flux))
        ]

    one = apply(src, [(B2 - 1.0) * s for s in src])
    two = apply(one, [B1 * s - u for s, u in zip(src, one)])
    return apply(two, [B0 * s - u for s, u in zip(src, two)])


def inner_kernel(field, diff_i, diff_j, land, out, f, di, dj, ls, sems):
    kept = (f, di, dj, ls)
    start_land(land, ls, sems.at[6], ALL_ROWS)
    start_rows((field, diff_i, diff_j, land), kept, sems, ALL_ROWS)
    not_last = jnp.where(lanes() == C - 1, 0.0, 1.0)
    wait_for(ls.at[:, pl.ds(0, L)], sems.at[6])

    def tile(t, k):
        def emit(r, value):
            out[r - 3, pl.ds(pl.multiple_of(8 * t, 8), 8), :] = value

        stream(3, R - 3, lambda r: cell(kept, t, k, r), emit, not_last)

    tiles(kept, sems, R, tile)


def finish_kernel(
    partner, field, diff_i, diff_j, land, inner, mix, strips,
    recv_a, recv_b, near, far, recv_e, recv_o, recv_x,
    out, north, south, north_halo, east, west, fold, diffused, mixed,
    f, di, dj, ls, sems, got, out_sem,
):
    i_odd, j_odd = parities()
    at_top = lax.axis_index("ja") == 3
    at_bottom = lax.axis_index("ja") == 0
    shift = partner[0] & (C - 1)
    kept = (f, di, dj, ls)
    start_land(land, ls, sems.at[6], ALL_ROWS)
    start_rows((field, diff_i, diff_j, land), kept, sems, EDGE_ROWS)

    def choose(flag, first, second, to, sem):
        @pl.when(flag)
        def _():
            pltpu.make_async_copy(first, to, sem).start()

        @pl.when(jnp.logical_not(flag))
        def _():
            pltpu.make_async_copy(second, to, sem).start()

    choose(i_odd, recv_o, recv_e, east, got.at[0])
    choose(i_odd, recv_e, recv_o, west, got.at[1])
    choose(j_odd, recv_a, recv_b, south, got.at[3])

    @pl.when(at_top)
    def _():
        pltpu.make_async_copy(near, north, got.at[2]).start()

    @pl.when(jnp.logical_not(at_top))
    def _():
        choose(j_odd, recv_b, recv_a, north, got.at[2])

    fold_copy = pltpu.make_async_copy(far, fold, got.at[4])
    fold_copy.start()
    inner_copy = pltpu.make_async_copy(inner, diffused.at[pl.ds(3, R - 6)], got.at[5])
    inner_copy.start()
    for j, ref in enumerate((east, west, north, south)):
        wait_for(ref, got.at[j])
    fold_copy.wait()

    wide = lanes(DEPTH)
    wide_slot = slot_of(wide)

    @pl.when(at_top)
    def _():
        index = (shift - wide) & (C - 1)
        inside = wide <= shift
        beyond = ((shift <= 1) & (wide >= C - 2)) | ((shift >= C - 3) & (wide <= 2))

        def ghost(g, carry):
            one, two, three = north[g], fold[g], roll(recv_x[...], -16 * g)
            own = jnp.where(inside, one, two)
            other = jnp.where(beyond, three, jnp.where(inside, two, one))
            north[g] = jnp.take_along_axis(own, index, axis=1)
            other = roll(jnp.take_along_axis(other, index, axis=1), 16 * g)
            north_halo[...] = jnp.where(wide_slot == g, other, north_halo[...])
            return carry

        lax.fori_loop(0, 8, ghost, 0)

    @pl.when(at_bottom)
    def _():
        south[...] = jnp.zeros_like(south)

    lane = lanes()
    in_slot = lane & 15
    slot = slot_of(lane)
    not_last = jnp.where(lane == C - 1, 0.0, 1.0)
    seam = (lane < 3) | (lane >= C - 3)
    sublane = lax.broadcasted_iota(jnp.int32, (8, C), 0)
    zero = jnp.zeros((8, C), jnp.float32)
    wait_for(ls.at[:, pl.ds(0, L)], sems.at[6])
    inner_copy.wait()

    def tile(t, k):
        rows = pl.ds(pl.multiple_of(8 * t, 8), 8)
        real = 8 * k + sublane < L

        def ghost(r):
            planes, far = (south, -r) if r < 0 else (north, r - R + 1)
            pick = lambda g: planes[g, rows, :]
            return (pick(far - 1), pick(far + 2) if far <= 2 else None, pick(far + 4))

        left = [[None] * PLANES for _ in range(3)]
        right = [[None] * PLANES for _ in range(3)]
        for a in range(3):
            got_east, got_west = east[a, rows, :], west[a, rows, :]
            for p in range(PLANES):
                own = strips[a, p, rows, :]
                halo = jnp.where(in_slot < 8, roll(got_east, -3 * p), roll(got_west, 3 * p))
                for r in (-3, -2, -1, R, R + 1, R + 2):
                    at, plane = place(r)
                    if plane != p:
                        continue
                    far = -r if r < 0 else r - R + 1
                    mine, theirs = zero, zero
                    if (a, far) in GHOST:
                        g = GHOST.index((a, far))
                        mine = roll((south if r < 0 else north)[g, rows, :], 16 * at)
                        theirs = roll(north_halo[rows, :], 16 * (at - g))
                    here = slot == at
                    own = jnp.where(here, mine, own)
                    if r >= R:
                        halo = jnp.where(here & at_top, theirs, halo)
                left[a][p] = jnp.where(in_slot >= 13, halo, own)
                right[a][p] = jnp.where(in_slot < 3, halo, own)
        left = strip_rows(*left)
        right = strip_rows(*right)
        fixed = [jnp.where(in_slot < 8, x, y) for x, y in zip(left, right)]

        def emit(r, value):
            at, p = place(r)
            value = jnp.where(seam, roll(fixed[p], -16 * at), value)
            diffused[r, rows, :] = jnp.where(real, value, 0.0)

        data = lambda r: cell(kept, t, k, r) if 0 <= r < R else ghost(r)
        stream(0, 3, data, emit, not_last)
        stream(R - 3, R, data, emit, not_last)
        for r in range(3, R - 3):
            emit(r, diffused[r, rows, :])

    tiles(kept, sems, 2 * EDGE, tile)

    for v in range(V):
        at = pl.ds(v * SLOTS, SLOTS)

        def pair_of_rows(pair, carry):
            values = jnp.concatenate([diffused[2 * pair, at], diffused[2 * pair + 1, at]], axis=1)
            high = values.astype(jnp.bfloat16)
            rest = (values - high.astype(jnp.float32)).astype(jnp.bfloat16)
            stacked = jnp.concatenate([high, rest, high], axis=0)
            result = jnp.dot(mix[v], stacked, preferred_element_type=jnp.float32)
            for side in range(2):
                r = 2 * pair + side
                mixed[r, at] = result[:, side * C : (side + 1) * C] * ls[r].astype(jnp.float32)
                pltpu.make_async_copy(mixed.at[r, pl.ds(v * SLOTS, L)], out.at[v, :, r], out_sem.at[v]).start()
            return carry

        lax.fori_loop(0, R // 2, pair_of_rows, 0, unroll=2)

    for v in range(V):
        wait_for(mixed.at[:, pl.ds(v * SLOTS, L)], out_sem.at[v])


def odd_partner(i, count):
    return (((i - 1) % count) ^ 1) + 1


def body(field, diff_i, diff_j, land_sea, partner, vertical):
    count = lax.axis_size("ia")
    raw = (field, diff_i, diff_j, land_sea)
    hbm = pl.BlockSpec(memory_space=pltpu.HBM)
    vmem = pl.BlockSpec(memory_space=pltpu.VMEM)
    planes = lambda *n: jax.ShapeDtypeStruct(n + (DEPTH, C), jnp.float32)
    scratch = lambda *n: pltpu.VMEM(n + (DEPTH, C), jnp.float32)
    big = pltpu.CompilerParams(vmem_limit_bytes=48 * 2**20)

    def cost(flops, size):
        return pl.CostEstimate(flops=flops, bytes_accessed=size, transcendentals=0)

    send_a, send_b, send_x = pl.pallas_call(
        rows_kernel,
        in_specs=[hbm] * 4,
        out_specs=[vmem] * 3,
        out_shape=[planes(8), planes(8), planes()],
        scratch_shapes=RAW_SCRATCH,
        compiler_params=big,
        name="pack_rows",
    )(*raw)
    columns_e, columns_o, strips = pl.pallas_call(
        columns_kernel,
        in_specs=[hbm] * 4,
        out_specs=[vmem] * 3,
        out_shape=[planes(3), planes(3), planes(3, PLANES)],
        scratch_shapes=RAW_SCRATCH,
        compiler_params=big,
        cost_estimate=cost(10**8, 16 * 10**6),
        name="pack_columns",
    )(*raw)

    both = ("ia", "ja")
    rows_a = [(0, 1), (1, 0), (2, 3), (3, 2)]
    rows_b = [(1, 2), (2, 1)]
    even = [(i, i ^ 1) for i in range(count)]
    odd = [(i, odd_partner(i, count) % count) for i in range(count)]

    def fold(q):
        return [(t * 4 + 3, ((q - t) % count) * 4 + 3) for t in range(count)]

    centre = partner[0]
    block, shift = lax.shift_right_logical(centre, 7), centre & (C - 1)

    def mirror(x, q):
        return lax.ppermute(x, both, fold(q))

    def third_block(x):
        turn = jnp.where(shift <= 1, block - 2, block + 1)
        x = mirror(x, 0)
        for bit in range((count - 1).bit_length()):
            rotate = functools.partial(lambda y, step: mirror(mirror(y, 0), step), step=2**bit)
            x = lax.cond((turn >> bit) & 1 == 1, rotate, lambda y: y, x)
        return x

    recv_x = lax.cond((shift <= 1) | (shift >= C - 3), third_block, lambda x: x, send_x)

    mix = jnp.pad(vertical * np.float32(LEAD), ((0, 0), (0, SLOTS - L), (0, SLOTS - L)))
    high = lax.reduce_precision(mix, 8, 7)
    weights = jnp.concatenate([high, high, mix - high], axis=2).astype(jnp.bfloat16)

    recv_a = lax.ppermute(send_a, "ja", rows_a)
    recv_b = lax.ppermute(send_b, "ja", rows_b)
    send_e, send_o = pl.pallas_call(
        ghost_kernel,
        in_specs=[vmem] * 4,
        out_specs=[vmem] * 2,
        out_shape=[planes(3), planes(3)],
        name="pack_ghost_columns",
    )(columns_e, columns_o, recv_a, recv_b)
    recv_e = lax.ppermute(send_e, "ia", even)
    recv_o = lax.ppermute(send_o, "ia", odd)

    def fold_and_inner(q, send_b, raw):
        near = lax.ppermute(send_b, both, fold(q))
        far = lax.ppermute(send_b, both, fold((q - 1) % count))
        inner = pl.pallas_call(
            inner_kernel,
            in_specs=[hbm] * 4,
            out_specs=vmem,
            out_shape=planes(R - 6),
            scratch_shapes=RAW_SCRATCH,
            compiler_params=big,
            cost_estimate=cost(2 * 10**8, 16 * 10**6),
            name="inner",
        )(*raw)
        return near, far, inner

    near, far, inner = lax.switch(
        block, [functools.partial(fold_and_inner, q) for q in range(count)], send_b, raw
    )
    return pl.pallas_call(
        finish_kernel,
        in_specs=[pl.BlockSpec(memory_space=pltpu.SMEM)] + [hbm] * 5 + [vmem] * 2 + [hbm] * 6 + [vmem],
        out_specs=hbm,
        out_shape=jax.ShapeDtypeStruct((V, L, R, C), jnp.float32),
        scratch_shapes=[
            scratch(8), scratch(8), scratch(), scratch(3), scratch(3), scratch(8),
            scratch(R), scratch(R),
        ] + RAW_SCRATCH + [pltpu.SemaphoreType.DMA((6,)), pltpu.SemaphoreType.DMA((V,))],
        compiler_params=big,
        name="finish",
    )(
        partner, *raw, inner, weights, strips,
        recv_a, recv_b, near, far, recv_e, recv_o, recv_x,
    )


def solution(mesh):
    placed = (
        P(None, None, "ja", "ia"),
        P(None, None, "ja", "ia"),
        P(None, None, "ja", "ia"),
        P(None, "ja", "ia"),
        P(),
        P(),
    )
    return jax.shard_map(
        body, mesh=mesh, in_specs=placed, out_specs=P(None, None, "ja", "ia"), check_vma=False
    )
```

time: 449 us -> 80.5 us (0.18)
  waiting for transfers between devices: 193 us -> 1.42 us
  local copies, waits for them, and re-layouts: 100 us -> 3.01 us
  other arithmetic: 61.2 us -> 0.13 us
  Pallas kernels: 0 us -> 59.3 us
  starting transfers between devices: 54.8 us -> 13.7 us
  matrix products: 23.8 us -> 0 us
  between operations: 13.4 us -> 1.59 us
    all_gather x4 -> x0, waiting for transfers between devices: 192 us -> none  [folded(): full_row = lax.all_gather(level_rows, 'ia', axis=1, tiled=True)]
    pallas_call x0 -> x5, Pallas kernels: none -> 59.3 us  [the longest x1 23.2 us: body(): pl.pallas_call(finish_kernel, in_specs=[pl.BlockSpec(memory_space=pltpu.S...]
    slice x17 -> x1, local copies, waits for them, and re-layouts: 53.9 us -> 0.52 us  [body(): centre = partner[0]]
    ppermute x16 -> x6, starting transfers between devices: 54.7 us -> 13.7 us  [the longest x1 6.25 us: body(): recv_o = lax.ppermute(send_o, 'ia', odd)]
    add x2 -> x0, other arithmetic: 33.2 us -> none  [body(): direction = residual + momentum * direction]
    dot_general x1 -> x0, matrix products: 23.8 us -> none  [body(): jnp.einsum('vlm,vmji->vlji', vertical, iterate, precision=lax.Precision.H...]
    ppermute x8 -> x0, local copies, waits for them, and re-layouts: 21 us -> none  [the longest x4 10.5 us: with_halo(): lax.ppermute(lax.slice_in_dim(block, block.shape[dim] - width, None, axis...]
    gather x6 -> x0, local copies, waits for them, and re-layouts: 15 us -> none  [folded(): fold_ghost = jnp.take(full_row, my_partners, axis=1)]
  transfers between devices with their start and end apart: 20 -> 6, of which waited for: 4 -> 1; matrix products, arithmetic and copies ran while one was open for 24% -> 1% of each run, Pallas kernels for 0% -> 37%
where the time goes in v1:
time: 80.5 us; the launch traced here: 79.5 us
  Pallas kernels  59.3 us (74%)
  starting transfers between devices  13.7 us (17%)
  local copies, waits for them, and re-layouts  3.01 us (4%)
  between operations  1.59 us (2%)
  waiting for transfers between devices  1.42 us (2%)
    pallas_call x1, Pallas kernels, body(): pl.pallas_call(finish_kernel, in_specs=[pl.BlockSpec(memory_space=pltpu.S...  23.2 us
    pallas_call x1, Pallas kernels, body(): pl.pallas_call(columns_kernel, in_specs=[hbm] * 4, out_specs=[vmem] * 3,...  15.1 us
    pallas_call x1, Pallas kernels, fold_and_inner(): pl.pallas_call(inner_kernel, in_specs=[hbm] * 4, out_specs=vmem, out_shap...  14.7 us
    ppermute x1, starting transfers between devices, body(): recv_o = lax.ppermute(send_o, 'ia', odd)  6.25 us
    pallas_call x1, Pallas kernels, body(): pl.pallas_call(rows_kernel, in_specs=[hbm] * 4, out_specs=[vmem] * 3, out...  3.22 us
    pallas_call x1, Pallas kernels, body(): pl.pallas_call(ghost_kernel, in_specs=[vmem] * 4, out_specs=[vmem] * 2, o...  3.2 us
    unnamed x26, local copies, waits for them, and re-layouts  2.49 us
    ppermute x1, starting transfers between devices, fold_and_inner(): far = lax.ppermute(send_b, both, fold((q - 1) % count))  2.21 us
  transfers between devices with their start and end apart: 6, of which 1 were waited for; matrix products, arithmetic and copies ran while one was open for 1% of the time, Pallas kernels for 37%

profile of v1, /device:TPU:3, one launch (start us, length us, event | category | flops | bytes accessed | tf_op | source)
XLA Modules:
  0.0 79.5 jit_solution(18107553831938100009)
XLA Ops:
  0.0 0.0 copy-start.10
  0.0 3.2 %pack_rows.1 = (f32[8,160,128]{2,1,0:T(8,128)S(1)}, f32[8,160,128]{2,1,0:T(8,128)S(1)}, f32[160,128]{1,0:T(8,128)S(1)}) custom-call(f32[2,75,32,128]{3,2,1,0:T(8,128)} %field.5, f32[2,75,32,128]{3,2,1,0:T(8,128)} %diff_i.5, f32[2,75,32,128]{3,2,1,0:T(8,128)} %diff_j.5, s32[75,32,128]{2,1,0:T(8,128)} %land.5), custom_call_target="tpu_custom_call" | custom-call | tf_op jit(solution)/shard_map/pack_rows/pallas_call | solution.py:485
  3.2 0.0 copy-start.12
  3.3 0.8 collective-permute-start.75
  4.0 0.8 %collective-permute-start.76 = (f32[8,160,128]{2,1,0:T(8,128)S(1)}, f32[8,160,128]{2,1,0:T(8,128)S(1)}, u32[]{:S(2)}, u32[]{:S(2)}) collective-permute-start(f32[8,160,128]{2,1,0:T(8,128)S(1)} %get-tuple-element.534), channel_id=1, source_target_pairs={{1,2},{2,1},{5,6},{6,5},{9,10},{10,9},{13,14},{14,13},{17,18},{18,... | collective-permute-start | bytes 1966088 | tf_op jit(solution)/shard_map/ppermute | solution.py:535
  4.8 0.0 copy-done.7
  4.9 0.0 copy-done.8
  4.9 0.0 copy-done.9
  4.9 0.0 copy-done.10
  4.9 15.1 %pack_columns.1 = (f32[3,160,128]{2,1,0:T(8,128)S(1)}, f32[3,160,128]{2,1,0:T(8,128)S(1)}, f32[3,5,160,128]{3,2,1,0:T(8,128)S(1)}) custom-call(f32[2,75,32,128]{3,2,1,0:T(8,128)S(1)} %copy-done.7, f32[2,75,32,128]{3,2,1,0:T(8,128)S(1)} %copy-done.8, f32[2,75,32,128]{3,2,1,0:T(8,128)S(1)} %copy-done.9, s32[75,32,128]{2,1,0:T(8,128)S(1)} %copy-done.10), custom_call_target="tpu_custom_call" | custom-call | flops 100000000 | bytes 16000000 | tf_op jit(solution)/shard_map/pack_columns/pallas_call | solution.py:494
  20.0 0.0 copy-done.12
  20.0 0.0 copy-start.4
  20.0 0.7 copy-done.4
  20.7 0.7 copy-done.5
  21.4 0.0 collective-permute-done.75.recv_a
  21.4 0.0 collective-permute-done.76.recv_b
  21.4 0.8 %copy-done = f32[8,160,128]{2,1,0:T(8,128)} copy-done((f32[8,160,128]{2,1,0:T(8,128)}, f32[8,160,128]{2,1,0:T(8,128)S(1)}, u32[]{:S(2)}) %copy-start) | copy-done | bytes 655384
  22.3 0.2 copy-done.2
  22.5 3.2 %pack_ghost_columns.1 = (f32[3,160,128]{2,1,0:T(8,128)}, f32[3,160,128]{2,1,0:T(8,128)}) custom-call(f32[3,160,128]{2,1,0:T(8,128)} %copy-done.4, f32[3,160,128]{2,1,0:T(8,128)} %copy-done.5, f32[8,160,128]{2,1,0:T(8,128)} %copy-done, f32[8,160,128]{2,1,0:T(8,128)} %copy-done.2), custom_call_target="tpu_custom_call" | custom-call | tf_op jit(solution)/shard_map/pack_ghost_columns/pallas_call | solution.py:536
  25.7 1.6 %collective-permute-start.77 = (f32[3,160,128]{2,1,0:T(8,128)}, f32[3,160,128]{2,1,0:T(8,128)S(1)}, u32[]{:S(2)}, u32[]{:S(2)}) collective-permute-start(f32[3,160,128]{2,1,0:T(8,128)} %get-tuple-element.542), channel_id=1, source_target_pairs={{0,4},{4,0},{8,12},{12,8},{16,20},{20,16},{24,28},{28,24},{32,36},... | collective-permute-start | bytes 737288 | tf_op jit(solution)/shard_map/ppermute | solution.py:543
  27.3 6.3 %collective-permute-start.78 = (f32[3,160,128]{2,1,0:T(8,128)}, f32[3,160,128]{2,1,0:T(8,128)S(1)}, u32[]{:S(2)}, u32[]{:S(2)}) collective-permute-start(f32[3,160,128]{2,1,0:T(8,128)} %get-tuple-element.543), channel_id=1, source_target_pairs={{0,124},{4,8},{8,4},{12,16},{16,12},{20,24},{24,20},{28,32},{32,28... | collective-permute-start | bytes 737288 | tf_op jit(solution)/shard_map/ppermute | solution.py:544
  33.6 0.5 slice.3
  35.4 20.6 %conditional.7 = (f32[8,160,128]{2,1,0:T(8,128)}, f32[8,160,128]{2,1,0:T(8,128)}, f32[26,160,128]{2,1,0:T(8,128)}) conditional(s32[]{:T(128)} %clamp.3, (f32[8,160,128]{2,1,0:T(8,128)}, f32[2,75,32,128]{3,2,1,0:T(8,128)}, f32[2,75,32,128]{3,2,1,0:T(8,128)}, f32[2,75,32,128]{3,2,1,0:T(8,128)}, ...), branch_computations={%region_0.0_spmd, %region_1.2_spmd, %region_2.0_spmd, %region_3.0_... | conditional | flops 200000000 | bytes 21242984 | solution.py:561
  35.6 2.1 %collective-permute-start.44 = (f32[8,160,128]{2,1,0:T(8,128)}, f32[8,160,128]{2,1,0:T(8,128)}, u32[]{:S(2)}, u32[]{:S(2)}) collective-permute-start(f32[8,160,128]{2,1,0:T(8,128)} %get-tuple-element.470), channel_id=1, source_target_pairs={{3,91},{7,87},{11,83},{15,79},{19,75},{23,71},{27,67},{31,63},{35,... | collective-permute-start | bytes 1966088 | tf_op jit(solution)/shard_map/cond/branch_22_fun/ppermute | solution.py:547
  37.7 2.2 %collective-permute-start.45 = (f32[8,160,128]{2,1,0:T(8,128)}, f32[8,160,128]{2,1,0:T(8,128)}, u32[]{:S(2)}, u32[]{:S(2)}) collective-permute-start(f32[8,160,128]{2,1,0:T(8,128)} %get-tuple-element.470), channel_id=1, source_target_pairs={{3,87},{7,83},{11,79},{15,75},{19,71},{23,67},{27,63},{31,59},{35,... | collective-permute-start | bytes 1966088 | tf_op jit(solution)/shard_map/cond/branch_22_fun/ppermute | solution.py:548
  39.9 14.7 %inner.54 = f32[26,160,128]{2,1,0:T(8,128)} custom-call(f32[2,75,32,128]{3,2,1,0:T(8,128)} %get-tuple-element.471.field, f32[2,75,32,128]{3,2,1,0:T(8,128)} %get-tuple-element.472.diff_i, f32[2,75,32,128]{3,2,1,0:T(8,128)} %get-tuple-element.473.diff_j, s32[75,32,128]{2,1,0:T(8,128)} %get-tuple-element.474.land), custom_call_target="tpu_custom_call" | custom-call | flops 200000000 | bytes 16000000 | tf_op jit(solution)/shard_map/cond/branch_22_fun/inner/pallas_call | solution.py:549
  54.6 1.4 %collective-permute-done.44 = f32[8,160,128]{2,1,0:T(8,128)} collective-permute-done((f32[8,160,128]{2,1,0:T(8,128)}, f32[8,160,128]{2,1,0:T(8,128)}, u32[]{:S(2)}, u32[]{:S(2)}) %collective-permute-start.44) | collective-permute-done | bytes 655392 | tf_op jit(solution)/shard_map/cond/branch_22_fun/ppermute | solution.py:547
  56.0 0.0 collective-permute-done.45
  56.0 0.1 pad_maximum_fusion.mix
  56.1 0.0 collective-permute-done.77.recv_e
  56.1 0.0 collective-permute-done.78.recv_o
  56.2 23.2 %finish.1 = f32[2,75,32,128]{3,2,1,0:T(8,128)} custom-call(s32[4096]{0:T(1024)S(1)} %copy-done.6, f32[2,75,32,128]{3,2,1,0:T(8,128)} %field.5, f32[2,75,32,128]{3,2,1,0:T(8,128)} %diff_i.5, f32[2,75,32,128]{3,2,1,0:T(8,128)} %diff_j.5, s32[75,32,128]{2,1,0:T(8,128)} %land.5, f32[26,160,128]{2,1,0:T(8,128)} %get-tuple-element.535.inner, ...), custom_call_target="tpu_custom_call" | custom-call | tf_op jit(solution)/shard_map/finish/pallas_call | solution.py:564
  (17 shorter events, 0.1 us)
Async XLA Ops:
  0.0 4.8 %copy-start.7 = (f32[2,75,32,128]{3,2,1,0:T(8,128)S(1)}, f32[2,75,32,128]{3,2,1,0:T(8,128)}, u32[]{:S(2)}) copy-start(f32[2,75,32,128]{3,2,1,0:T(8,128)} %field.5) | copy-start | bytes 7372804
  0.0 4.9 %copy-start.8 = (f32[2,75,32,128]{3,2,1,0:T(8,128)S(1)}, f32[2,75,32,128]{3,2,1,0:T(8,128)}, u32[]{:S(2)}) copy-start(f32[2,75,32,128]{3,2,1,0:T(8,128)} %diff_i.5) | copy-start | bytes 7372804
  0.0 4.9 %copy-start.9 = (f32[2,75,32,128]{3,2,1,0:T(8,128)S(1)}, f32[2,75,32,128]{3,2,1,0:T(8,128)}, u32[]{:S(2)}) copy-start(f32[2,75,32,128]{3,2,1,0:T(8,128)} %diff_j.5) | copy-start | bytes 7372804
  0.0 4.9 %copy-start.10 = (s32[75,32,128]{2,1,0:T(8,128)S(1)}, s32[75,32,128]{2,1,0:T(8,128)}, u32[]{:S(2)}) copy-start(s32[75,32,128]{2,1,0:T(8,128)} %land.5) | copy-start | bytes 3686404
  3.2 16.8 %copy-start.12 = (f32[8,160,128]{2,1,0:T(8,128)}, f32[8,160,128]{2,1,0:T(8,128)S(1)}, u32[]{:S(2)}) copy-start(f32[8,160,128]{2,1,0:T(8,128)S(1)} %get-tuple-element.534) | copy-start | bytes 1966084
  3.3 18.2 %collective-permute-start.75 = (f32[8,160,128]{2,1,0:T(8,128)S(1)}, f32[8,160,128]{2,1,0:T(8,128)S(1)}, u32[]{:S(2)}, u32[]{:S(2)}) collective-permute-start(f32[8,160,128]{2,1,0:T(8,128)S(1)} %get-tuple-element.537), channel_id=1, source_target_pairs={{0,1},{1,0},{2,3},{3,2},{4,5},{5,4},{6,7},{7,6},{8,9},{9,8},{10,11... | collective-permute-start | bytes 1966088 | tf_op jit(solution)/shard_map/ppermute | solution.py:534
  4.0 29.6 %copy-start.11 = (f32[2,75,75]{2,0,1:T(2,128)S(1)}, f32[2,75,75]{2,0,1:T(2,128)}, u32[]{:S(2)}) copy-start(f32[2,75,75]{2,0,1:T(2,128)} %param.55) | copy-start | bytes 135004
  4.0 29.6 %copy-start.6 = (s32[4096]{0:T(1024)S(1)}, s32[4096]{0:T(1024)}, u32[]{:S(2)}) copy-start(s32[4096]{0:T(1024)} %partner.1) | copy-start | bytes 49156
  4.0 17.4 %collective-permute-start.76 = (f32[8,160,128]{2,1,0:T(8,128)S(1)}, f32[8,160,128]{2,1,0:T(8,128)S(1)}, u32[]{:S(2)}, u32[]{:S(2)}) collective-permute-start(f32[8,160,128]{2,1,0:T(8,128)S(1)} %get-tuple-element.534), channel_id=1, source_target_pairs={{1,2},{2,1},{5,6},{6,5},{9,10},{10,9},{13,14},{14,13},{17,18},{18,... | collective-permute-start | bytes 1966088 | tf_op jit(solution)/shard_map/ppermute | solution.py:535
  20.0 0.7 copy-start.4
  20.7 0.7 copy-start.5
  21.4 0.8 %copy-start = (f32[8,160,128]{2,1,0:T(8,128)}, f32[8,160,128]{2,1,0:T(8,128)S(1)}, u32[]{:S(2)}) copy-start(f32[8,160,128]{2,1,0:T(8,128)S(1)} %collective-permute-done.75.recv_a) | copy-start | bytes 1966084
  21.4 1.1 %copy-start.2 = (f32[8,160,128]{2,1,0:T(8,128)}, f32[8,160,128]{2,1,0:T(8,128)S(1)}, u32[]{:S(2)}) copy-start(f32[8,160,128]{2,1,0:T(8,128)S(1)} %collective-permute-done.76.recv_b) | copy-start | bytes 1966084
  25.7 30.4 %collective-permute-start.77 = (f32[3,160,128]{2,1,0:T(8,128)}, f32[3,160,128]{2,1,0:T(8,128)S(1)}, u32[]{:S(2)}, u32[]{:S(2)}) collective-permute-start(f32[3,160,128]{2,1,0:T(8,128)} %get-tuple-element.542), channel_id=1, source_target_pairs={{0,4},{4,0},{8,12},{12,8},{16,20},{20,16},{24,28},{28,24},{32,36},... | collective-permute-start | bytes 737288 | tf_op jit(solution)/shard_map/ppermute | solution.py:543
  27.3 28.8 %collective-permute-start.78 = (f32[3,160,128]{2,1,0:T(8,128)}, f32[3,160,128]{2,1,0:T(8,128)S(1)}, u32[]{:S(2)}, u32[]{:S(2)}) collective-permute-start(f32[3,160,128]{2,1,0:T(8,128)} %get-tuple-element.543), channel_id=1, source_target_pairs={{0,124},{4,8},{8,4},{12,16},{16,12},{20,24},{24,20},{28,32},{32,28... | collective-permute-start | bytes 737288 | tf_op jit(solution)/shard_map/ppermute | solution.py:544
  35.4 20.8 %copy-start.1 = (f32[8,160,128]{2,1,0:T(8,128)S(1)}, f32[8,160,128]{2,1,0:T(8,128)}, u32[]{:S(2)}) copy-start(f32[8,160,128]{2,1,0:T(8,128)} %copy-done) | copy-start | bytes 1966084
  35.4 20.8 %copy-start.3 = (f32[8,160,128]{2,1,0:T(8,128)S(1)}, f32[8,160,128]{2,1,0:T(8,128)}, u32[]{:S(2)}) copy-start(f32[8,160,128]{2,1,0:T(8,128)} %copy-done.2) | copy-start | bytes 1966084
  35.6 20.3 %collective-permute-start.44 = (f32[8,160,128]{2,1,0:T(8,128)}, f32[8,160,128]{2,1,0:T(8,128)}, u32[]{:S(2)}, u32[]{:S(2)}) collective-permute-start(f32[8,160,128]{2,1,0:T(8,128)} %get-tuple-element.470), channel_id=1, source_target_pairs={{3,91},{7,87},{11,83},{15,79},{19,75},{23,71},{27,67},{31,63},{35,... | collective-permute-start | bytes 1966088 | tf_op jit(solution)/shard_map/cond/branch_22_fun/ppermute | solution.py:547
  37.7 18.3 %collective-permute-start.45 = (f32[8,160,128]{2,1,0:T(8,128)}, f32[8,160,128]{2,1,0:T(8,128)}, u32[]{:S(2)}, u32[]{:S(2)}) collective-permute-start(f32[8,160,128]{2,1,0:T(8,128)} %get-tuple-element.470), channel_id=1, source_target_pairs={{3,87},{7,83},{11,79},{15,75},{19,71},{23,67},{27,63},{31,59},{35,... | collective-permute-start | bytes 1966088 | tf_op jit(solution)/shard_map/cond/branch_22_fun/ppermute | solution.py:548

commit v2 on v1

--- a/solution.py
+++ b/solution.py
@@ -10,8 +10,7 @@
 ITERS = 4
 diff_ceiling = 8.0
 V, L, R, C = 2, 75, 32, 128
-TILES = 10
-SLOTS = 8 * TILES
+SLOTS = 80
 DEPTH = V * SLOTS
 CENTRE, HALF = 33.0, 32.0
 ROOT_SCALE = 32.0**-0.5
@@ -62,7 +61,7 @@
     return divmod(r + 3, PLANES)
 
 
-def lanes(rows=8):
+def lanes(rows):
     return lax.broadcasted_iota(jnp.int32, (rows, C), 1)
 
 
@@ -120,10 +119,14 @@
     return x * lax.rsqrt(x)
 
 
-def cell(kept, t, k, r):
+def span(tall, t):
+    return pl.ds(pl.multiple_of(tall * t, 8), tall)
+
+
+def cell(kept, tall, t, r):
     f, di, dj, ls = kept
-    at = pl.ds(pl.multiple_of(8 * t, 8), 8)
-    wet = ls[r, pl.ds(pl.multiple_of(8 * k, 8), 8), :].astype(jnp.float32)
+    at = span(tall, t)
+    wet = ls[r, span(tall, lax.rem(t, SLOTS // tall)), :].astype(jnp.float32)
     scaled = wet * ROOT_SCALE
     return f[r, at, :] * wet, root(di[r, at, :]) * scaled, root(dj[r, at, :]) * scaled
 
@@ -138,18 +141,18 @@
 ALL_ROWS = [(0, R)]
 
 
-def tiles(kept, sems, count, tile):
+def tiles(kept, sems, count, tall, tile):
     def body(t, carry):
         for v in range(V):
 
-            @pl.when(t == v * TILES)
+            @pl.when(t == v * (SLOTS // tall))
             def _():
                 wait_rows(kept, sems, v, count)
 
-        tile(t, lax.rem(t, TILES))
+        tile(t)
         return carry
 
-    lax.fori_loop(0, DEPTH // 8, body, 0)
+    lax.fori_loop(0, DEPTH // tall, body, 0)
 
 
 EDGE = 6
@@ -159,6 +162,10 @@
 
 def wait_land(ls, sem, count):
     wait_for(ls.at[pl.ds(0, count), pl.ds(0, L)], sem)
+
+
+ROWS_TALL = 40
+COLUMNS_TALL = 40
 
 
 def rows_kernel(field, diff_i, diff_j, land, send_a, send_b, send_x, f, di, dj, ls, sems):
@@ -166,13 +173,13 @@
     kept = (f, di, dj, ls)
     start_land(land, ls, sems.at[6], OUTER_ROWS)
     start_rows((field, diff_i, diff_j, land), kept, sems, OUTER_ROWS)
-    slot = slot_of(lanes())
+    slot = slot_of(lanes(ROWS_TALL))
     wait_land(ls, sems.at[6], 6)
 
-    def tile(t, k):
-        rows = pl.ds(pl.multiple_of(8 * t, 8), 8)
-        edge = {r: cell(kept, t, k, r) for r in (0, 1, 2, R - 3, R - 2, R - 1)}
-        third = jnp.zeros((8, C), jnp.float32)
+    def tile(t):
+        rows = span(ROWS_TALL, t)
+        edge = {r: cell(kept, ROWS_TALL, t, r) for r in (0, 1, 2, R - 3, R - 2, R - 1)}
+        third = jnp.zeros((ROWS_TALL, C), jnp.float32)
         for g, (a, far) in enumerate(GHOST):
             top, bottom = edge[R - far][a], edge[far - 1][a]
             send_a[g, rows, :] = jnp.where(j_odd, bottom, top)
@@ -180,7 +187,7 @@
             third = jnp.where(slot == g, roll(top, 16 * g), third)
         send_x[rows, :] = third
 
-    tiles(kept, sems, 6, tile)
+    tiles(kept, sems, 6, ROWS_TALL, tile)
 
 
 def columns_kernel(
@@ -190,16 +197,16 @@
     kept = (f, di, dj, ls)
     start_land(land, ls, sems.at[6], ALL_ROWS)
     start_rows((field, diff_i, diff_j, land), kept, sems, ALL_ROWS)
-    lane = lanes()
+    lane = lanes(COLUMNS_TALL)
     slot = slot_of(lane)
     in_slot = lane & 15
     wait_land(ls, sems.at[6], R)
 
-    def tile(t, k):
-        rows = pl.ds(pl.multiple_of(8 * t, 8), 8)
-        packed = [[jnp.zeros((8, C), jnp.float32) for _ in range(PLANES)] for _ in range(3)]
+    def tile(t):
+        rows = span(COLUMNS_TALL, t)
+        packed = [[jnp.zeros((COLUMNS_TALL, C), jnp.float32) for _ in range(PLANES)] for _ in range(3)]
         for r in range(R):
-            values = cell(kept, t, k, r)
+            values = cell(kept, COLUMNS_TALL, t, r)
             index, p = place(r)
             for a in range(3):
                 packed[a][p] = jnp.where(slot == index, roll(values[a], 16 * index), packed[a][p])
@@ -213,10 +220,10 @@
             columns_e[a, rows, :] = jnp.where(i_odd, left, right)
             columns_o[a, rows, :] = jnp.where(i_odd, right, left)
 
-    tiles(kept, sems, R, tile)
-
-
-WIDE = 32
+    tiles(kept, sems, R, COLUMNS_TALL, tile)
+
+
+WIDE = 80
 
 
 def ghost_kernel(columns_e, columns_o, recv_a, recv_b, send_e, send_o):
@@ -303,26 +310,33 @@
     return apply(two, [B0 * s - u for s, u in zip(src, two)])
 
 
+INNER_TALL = 8
+
+
 def inner_kernel(field, diff_i, diff_j, land, out, f, di, dj, ls, sems):
     kept = (f, di, dj, ls)
     start_land(land, ls, sems.at[6], ALL_ROWS)
     start_rows((field, diff_i, diff_j, land), kept, sems, ALL_ROWS)
-    not_last = jnp.where(lanes() == C - 1, 0.0, 1.0)
+    not_last = jnp.where(lanes(INNER_TALL) == C - 1, 0.0, 1.0)
     wait_for(ls.at[:, pl.ds(0, L)], sems.at[6])
 
-    def tile(t, k):
+    def tile(t):
         def emit(r, value):
-            out[r - 3, pl.ds(pl.multiple_of(8 * t, 8), 8), :] = value
-
-        stream(3, R - 3, lambda r: cell(kept, t, k, r), emit, not_last)
-
-    tiles(kept, sems, R, tile)
+            out[r - 3, span(INNER_TALL, t), :] = value
+
+        stream(3, R - 3, lambda r: cell(kept, INNER_TALL, t, r), emit, not_last)
+
+    tiles(kept, sems, R, INNER_TALL, tile)
+
+
+STRIP_TALL = 40
+EDGE_TALL = 40
 
 
 def finish_kernel(
-    partner, field, diff_i, diff_j, land, inner, mix, strips,
+    partner, field, diff_i, diff_j, land, inner, vertical, strips,
     recv_a, recv_b, near, far, recv_e, recv_o, recv_x,
-    out, north, south, north_halo, east, west, fold, diffused, mixed,
+    out, north, south, north_halo, east, west, fold, own_strips, fixed, diffused, mixed, square, weights,
     f, di, dj, ls, sems, got, out_sem,
 ):
     i_odd, j_odd = parities()
@@ -330,8 +344,6 @@
     at_bottom = lax.axis_index("ja") == 0
     shift = partner[0] & (C - 1)
     kept = (f, di, dj, ls)
-    start_land(land, ls, sems.at[6], ALL_ROWS)
-    start_rows((field, diff_i, diff_j, land), kept, sems, EDGE_ROWS)
 
     def choose(flag, first, second, to, sem):
         @pl.when(flag)
@@ -349,24 +361,38 @@
     @pl.when(at_top)
     def _():
         pltpu.make_async_copy(near, north, got.at[2]).start()
+        pltpu.make_async_copy(far, fold, got.at[4]).start()
 
     @pl.when(jnp.logical_not(at_top))
     def _():
         choose(j_odd, recv_b, recv_a, north, got.at[2])
 
-    fold_copy = pltpu.make_async_copy(far, fold, got.at[4])
-    fold_copy.start()
+    strips_copy = pltpu.make_async_copy(strips, own_strips, got.at[6])
+    strips_copy.start()
+    start_rows((field, diff_i, diff_j, land), kept, sems, EDGE_ROWS)
+    start_land(land, ls, sems.at[6], ALL_ROWS)
     inner_copy = pltpu.make_async_copy(inner, diffused.at[pl.ds(3, R - 6)], got.at[5])
     inner_copy.start()
+
+    square[...] = jnp.zeros_like(square)
+    for v in range(V):
+        square[v, pl.ds(0, L), pl.ds(0, L)] = vertical[:, v, :] * np.float32(LEAD)
+        high = square[v].astype(jnp.bfloat16).astype(jnp.float32)
+        rest = square[v] - high
+        pad = jnp.zeros_like(high)
+        high = jnp.concatenate([high, pad], axis=1)
+        rest = jnp.concatenate([rest, pad], axis=1)
+        both = high + pltpu.roll(high, SLOTS, 1) + pltpu.roll(rest, 2 * SLOTS, 1)
+        weights[v] = both.astype(jnp.bfloat16)
+
     for j, ref in enumerate((east, west, north, south)):
         wait_for(ref, got.at[j])
-    fold_copy.wait()
-
-    wide = lanes(DEPTH)
-    wide_slot = slot_of(wide)
 
     @pl.when(at_top)
     def _():
+        wait_for(fold, got.at[4])
+        wide = lanes(DEPTH)
+        wide_slot = slot_of(wide)
         index = (shift - wide) & (C - 1)
         inside = wide <= shift
         beyond = ((shift <= 1) & (wide >= C - 2)) | ((shift >= C - 3) & (wide <= 2))
@@ -386,74 +412,91 @@
     def _():
         south[...] = jnp.zeros_like(south)
 
-    lane = lanes()
+    strips_copy.wait()
+    lane = lanes(STRIP_TALL)
     in_slot = lane & 15
     slot = slot_of(lane)
-    not_last = jnp.where(lane == C - 1, 0.0, 1.0)
-    seam = (lane < 3) | (lane >= C - 3)
-    sublane = lax.broadcasted_iota(jnp.int32, (8, C), 0)
-    zero = jnp.zeros((8, C), jnp.float32)
-    wait_for(ls.at[:, pl.ds(0, L)], sems.at[6])
-    inner_copy.wait()
-
-    def tile(t, k):
-        rows = pl.ds(pl.multiple_of(8 * t, 8), 8)
-        real = 8 * k + sublane < L
-
-        def ghost(r):
-            planes, far = (south, -r) if r < 0 else (north, r - R + 1)
-            pick = lambda g: planes[g, rows, :]
-            return (pick(far - 1), pick(far + 2) if far <= 2 else None, pick(far + 4))
-
-        left = [[None] * PLANES for _ in range(3)]
-        right = [[None] * PLANES for _ in range(3)]
+    zero = jnp.zeros((STRIP_TALL, C), jnp.float32)
+
+    def strip_tile(n, carry):
+        t, side = n >> 1, n & 1
+        rows = span(STRIP_TALL, t)
+        outside = ((side == 0) & (in_slot >= 13)) | ((side == 1) & (in_slot < 3))
+        packed = [[None] * PLANES for _ in range(3)]
         for a in range(3):
             got_east, got_west = east[a, rows, :], west[a, rows, :]
             for p in range(PLANES):
-                own = strips[a, p, rows, :]
+                own = own_strips[a, p, rows, :]
                 halo = jnp.where(in_slot < 8, roll(got_east, -3 * p), roll(got_west, 3 * p))
                 for r in (-3, -2, -1, R, R + 1, R + 2):
                     at, plane = place(r)
                     if plane != p:
                         continue
-                    far = -r if r < 0 else r - R + 1
+                    far_off = -r if r < 0 else r - R + 1
                     mine, theirs = zero, zero
-                    if (a, far) in GHOST:
-                        g = GHOST.index((a, far))
+                    if (a, far_off) in GHOST:
+                        g = GHOST.index((a, far_off))
                         mine = roll((south if r < 0 else north)[g, rows, :], 16 * at)
                         theirs = roll(north_halo[rows, :], 16 * (at - g))
                     here = slot == at
                     own = jnp.where(here, mine, own)
                     if r >= R:
                         halo = jnp.where(here & at_top, theirs, halo)
-                left[a][p] = jnp.where(in_slot >= 13, halo, own)
-                right[a][p] = jnp.where(in_slot < 3, halo, own)
-        left = strip_rows(*left)
-        right = strip_rows(*right)
-        fixed = [jnp.where(in_slot < 8, x, y) for x, y in zip(left, right)]
+                packed[a][p] = jnp.where(outside, halo, own)
+        for p, value in enumerate(strip_rows(*packed)):
+            fixed[side, p, rows, :] = value
+        return carry
+
+    lax.fori_loop(0, 2 * (DEPTH // STRIP_TALL), strip_tile, 0)
+
+    not_last = jnp.where(lanes(EDGE_TALL) == C - 1, 0.0, 1.0)
+    wait_land(ls, sems.at[6], R)
+
+    def edge_tile(t, low):
+        rows = span(EDGE_TALL, t)
+
+        def ghost(r):
+            planes, far_off = (south, -r) if r < 0 else (north, r - R + 1)
+            pick = lambda g: planes[g, rows, :]
+            return (pick(far_off - 1), pick(far_off + 2) if far_off <= 2 else None, pick(far_off + 4))
 
         def emit(r, value):
-            at, p = place(r)
-            value = jnp.where(seam, roll(fixed[p], -16 * at), value)
-            diffused[r, rows, :] = jnp.where(real, value, 0.0)
-
-        data = lambda r: cell(kept, t, k, r) if 0 <= r < R else ghost(r)
-        stream(0, 3, data, emit, not_last)
-        stream(R - 3, R, data, emit, not_last)
-        for r in range(3, R - 3):
-            emit(r, diffused[r, rows, :])
-
-    tiles(kept, sems, 2 * EDGE, tile)
+            diffused[r, rows, :] = value
+
+        data = lambda r: cell(kept, EDGE_TALL, t, r) if 0 <= r < R else ghost(r)
+        stream(low, low + 3, data, emit, not_last)
+
+    tiles(kept, sems, 2 * EDGE, EDGE_TALL, lambda t: edge_tile(t, 0))
+
+    def upper(t, carry):
+        edge_tile(t, R - 3)
+        return carry
+
+    lax.fori_loop(0, DEPTH // EDGE_TALL, upper, 0)
+    inner_copy.wait()
+
+    wide = lanes(SLOTS)
+    from_left = (wide & 15) < 8
+    seam = (wide < 3) | (wide >= C - 3)
+    real = lax.broadcasted_iota(jnp.int32, (SLOTS, C), 0) < L
+    tail = jnp.zeros((2 * C - 3 * SLOTS, 2 * C), jnp.bfloat16)
 
     for v in range(V):
         at = pl.ds(v * SLOTS, SLOTS)
 
         def pair_of_rows(pair, carry):
-            values = jnp.concatenate([diffused[2 * pair, at], diffused[2 * pair + 1, at]], axis=1)
+            halves = []
+            for side in range(2):
+                r = 2 * pair + side
+                place_of = lax.div(r + 3, PLANES)
+                p = r + 3 - PLANES * place_of
+                columns = roll(jnp.where(from_left, fixed[0, p, at], fixed[1, p, at]), -16 * place_of)
+                halves.append(jnp.where(real, jnp.where(seam, columns, diffused[r, at]), 0.0))
+            values = jnp.concatenate(halves, axis=1)
             high = values.astype(jnp.bfloat16)
             rest = (values - high.astype(jnp.float32)).astype(jnp.bfloat16)
-            stacked = jnp.concatenate([high, rest, high], axis=0)
-            result = jnp.dot(mix[v], stacked, preferred_element_type=jnp.float32)
+            stacked = jnp.concatenate([high, rest, high, tail], axis=0)
+            result = jnp.dot(weights[v], stacked, preferred_element_type=jnp.float32)
             for side in range(2):
                 r = 2 * pair + side
                 mixed[r, at] = result[:, side * C : (side + 1) * C] * ls[r].astype(jnp.float32)
@@ -477,7 +520,7 @@
     vmem = pl.BlockSpec(memory_space=pltpu.VMEM)
     planes = lambda *n: jax.ShapeDtypeStruct(n + (DEPTH, C), jnp.float32)
     scratch = lambda *n: pltpu.VMEM(n + (DEPTH, C), jnp.float32)
-    big = pltpu.CompilerParams(vmem_limit_bytes=48 * 2**20)
+    big = pltpu.CompilerParams(vmem_limit_bytes=60 * 2**20)
 
     def cost(flops, size):
         return pl.CostEstimate(flops=flops, bytes_accessed=size, transcendentals=0)
@@ -527,10 +570,6 @@
 
     recv_x = lax.cond((shift <= 1) | (shift >= C - 3), third_block, lambda x: x, send_x)
 
-    mix = jnp.pad(vertical * np.float32(LEAD), ((0, 0), (0, SLOTS - L), (0, SLOTS - L)))
-    high = lax.reduce_precision(mix, 8, 7)
-    weights = jnp.concatenate([high, high, mix - high], axis=2).astype(jnp.bfloat16)
-
     recv_a = lax.ppermute(send_a, "ja", rows_a)
     recv_b = lax.ppermute(send_b, "ja", rows_b)
     send_e, send_o = pl.pallas_call(
@@ -563,17 +602,18 @@
     )
     return pl.pallas_call(
         finish_kernel,
-        in_specs=[pl.BlockSpec(memory_space=pltpu.SMEM)] + [hbm] * 5 + [vmem] * 2 + [hbm] * 6 + [vmem],
+        in_specs=[pl.BlockSpec(memory_space=pltpu.SMEM)] + [hbm] * 5 + [vmem] + [hbm] * 7 + [vmem],
         out_specs=hbm,
         out_shape=jax.ShapeDtypeStruct((V, L, R, C), jnp.float32),
         scratch_shapes=[
             scratch(8), scratch(8), scratch(), scratch(3), scratch(3), scratch(8),
-            scratch(R), scratch(R),
-        ] + RAW_SCRATCH + [pltpu.SemaphoreType.DMA((6,)), pltpu.SemaphoreType.DMA((V,))],
+            scratch(3, PLANES), scratch(2, PLANES), scratch(R), scratch(R),
+            pltpu.VMEM((V, SLOTS, C), jnp.float32), pltpu.VMEM((V, SLOTS, 2 * C), jnp.bfloat16),
+        ] + RAW_SCRATCH + [pltpu.SemaphoreType.DMA((7,)), pltpu.SemaphoreType.DMA((V,))],
         compiler_params=big,
         name="finish",
     )(
-        partner, *raw, inner, weights, strips,
+        partner, *raw, inner, jnp.swapaxes(vertical, 0, 1), strips,
         recv_a, recv_b, near, far, recv_e, recv_o, recv_x,
     )
 

time: 80.5 us -> 70.4 us (0.87)
  Pallas kernels: 59.3 us -> 49.5 us
  starting transfers between devices: 13.7 us -> 15.1 us
  local copies, waits for them, and re-layouts: 3.01 us -> 1.94 us
    pallas_call x1, Pallas kernels: 15.1 us -> 8.71 us  [body(): pl.pallas_call(columns_kernel, in_specs=[hbm] * 4, out_specs=[vmem] * 3,...]
    pallas_call x1, Pallas kernels: 23.2 us -> 19.7 us  [body(): pl.pallas_call(finish_kernel, in_specs=[pl.BlockSpec(memory_space=pltpu.S...]
    unnamed x26 -> x8, local copies, waits for them, and re-layouts: 2.49 us -> 0.78 us
    ppermute x1, starting transfers between devices: 2.21 us -> 3.04 us  [fold_and_inner(): far = lax.ppermute(send_b, both, fold((q - 1) % count))]
  transfers between devices with their start and end apart: 6 -> 6, of which waited for: 1 -> 1; matrix products, arithmetic and copies ran while one was open for 1% -> 2% of each run, Pallas kernels for 37% -> 34%
where the time goes in v2:
time: 70.4 us; the launch traced here: 69.2 us
  Pallas kernels  49.5 us (70%)
  starting transfers between devices  15.1 us (21%)
  local copies, waits for them, and re-layouts  1.94 us (3%)
  between operations  1.34 us (2%)
  waiting for transfers between devices  1.08 us (2%)
    pallas_call x1, Pallas kernels, body(): pl.pallas_call(finish_kernel, in_specs=[pl.BlockSpec(memory_space=pltpu.S...  19.7 us
    pallas_call x1, Pallas kernels, fold_and_inner(): pl.pallas_call(inner_kernel, in_specs=[hbm] * 4, out_specs=vmem, out_shap...  15 us
    pallas_call x1, Pallas kernels, body(): pl.pallas_call(columns_kernel, in_specs=[hbm] * 4, out_specs=[vmem] * 3,...  8.71 us
    ppermute x1, starting transfers between devices, body(): recv_o = lax.ppermute(send_o, 'ia', odd)  6.25 us
    ppermute x1, starting transfers between devices, fold_and_inner(): far = lax.ppermute(send_b, both, fold((q - 1) % count))  3.04 us
    pallas_call x1, Pallas kernels, body(): pl.pallas_call(ghost_kernel, in_specs=[vmem] * 4, out_specs=[vmem] * 2, o...  3.02 us
    pallas_call x1, Pallas kernels, body(): pl.pallas_call(rows_kernel, in_specs=[hbm] * 4, out_specs=[vmem] * 3, out...  3.01 us
    ppermute x1, starting transfers between devices, fold_and_inner(): near = lax.ppermute(send_b, both, fold(q))  1.92 us
  transfers between devices with their start and end apart: 6, of which 1 were waited for; matrix products, arithmetic and copies ran while one was open for 2% of the time, Pallas kernels for 34%

profile of v2, /device:TPU:3, one launch (start us, length us, event | category | flops | bytes accessed | tf_op | source)
XLA Modules:
  0.0 69.2 jit_solution(11865627427281384376)
XLA Ops:
  0.0 0.0 copy-start
  0.0 0.0 copy-start.1
  0.0 3.0 %pack_rows.1 = (f32[8,160,128]{2,1,0:T(8,128)}, f32[8,160,128]{2,1,0:T(8,128)}, f32[160,128]{1,0:T(8,128)S(1)}) custom-call(f32[2,75,32,128]{3,2,1,0:T(8,128)} %field.5, f32[2,75,32,128]{3,2,1,0:T(8,128)} %diff_i.5, f32[2,75,32,128]{3,2,1,0:T(8,128)} %diff_j.5, s32[75,32,128]{2,1,0:T(8,128)} %land.5), custom_call_target="tpu_custom_call" | custom-call | tf_op jit(solution)/shard_map/pack_rows/pallas_call | solution.py:528
  3.0 0.8 %collective-permute-start.75 = (f32[8,160,128]{2,1,0:T(8,128)}, f32[8,160,128]{2,1,0:T(8,128)}, u32[]{:S(2)}, u32[]{:S(2)}) collective-permute-start(f32[8,160,128]{2,1,0:T(8,128)} %get-tuple-element.537), channel_id=1, source_target_pairs={{0,1},{1,0},{2,3},{3,2},{4,5},{5,4},{6,7},{7,6},{8,9},{9,8},{10,11... | collective-permute-start | bytes 1966088 | tf_op jit(solution)/shard_map/ppermute | solution.py:573
  3.8 1.5 %collective-permute-start.76 = (f32[8,160,128]{2,1,0:T(8,128)}, f32[8,160,128]{2,1,0:T(8,128)}, u32[]{:S(2)}, u32[]{:S(2)}) collective-permute-start(f32[8,160,128]{2,1,0:T(8,128)} %get-tuple-element.534), channel_id=1, source_target_pairs={{1,2},{2,1},{5,6},{6,5},{9,10},{10,9},{13,14},{14,13},{17,18},{18,... | collective-permute-start | bytes 1966088 | tf_op jit(solution)/shard_map/ppermute | solution.py:574
  5.3 0.0 copy-done
  5.3 0.0 copy-done.1
  5.3 8.7 %pack_columns.1 = (f32[3,160,128]{2,1,0:T(8,128)}, f32[3,160,128]{2,1,0:T(8,128)}, f32[3,5,160,128]{3,2,1,0:T(8,128)}) custom-call(f32[2,75,32,128]{3,2,1,0:T(8,128)S(1)} %copy-done, f32[2,75,32,128]{3,2,1,0:T(8,128)} %diff_i.5, f32[2,75,32,128]{3,2,1,0:T(8,128)} %diff_j.5, s32[75,32,128]{2,1,0:T(8,128)S(1)} %copy-done.1), custom_call_target="tpu_custom_call" | custom-call | flops 100000000 | bytes 16000000 | tf_op jit(solution)/shard_map/pack_columns/pallas_call | solution.py:537
  14.0 0.0 collective-permute-done.75.recv_a
  14.0 0.0 collective-permute-done.76.recv_b
  14.0 3.0 %pack_ghost_columns.1 = (f32[3,160,128]{2,1,0:T(8,128)}, f32[3,160,128]{2,1,0:T(8,128)}) custom-call(f32[3,160,128]{2,1,0:T(8,128)} %get-tuple-element.540.columns_e, f32[3,160,128]{2,1,0:T(8,128)} %get-tuple-element.541.columns_o, f32[8,160,128]{2,1,0:T(8,128)} %collective-permute-done.75.recv_a, f32[8,160,128]{2,1,0:T(8,128)} %collective-permute-done.76.recv_b), custom_call_target="tpu_custom_call" | custom-call | tf_op jit(solution)/shard_map/pack_ghost_columns/pallas_call | solution.py:575
  17.0 1.6 %collective-permute-start.77 = (f32[3,160,128]{2,1,0:T(8,128)}, f32[3,160,128]{2,1,0:T(8,128)S(1)}, u32[]{:S(2)}, u32[]{:S(2)}) collective-permute-start(f32[3,160,128]{2,1,0:T(8,128)} %get-tuple-element.542), channel_id=1, source_target_pairs={{0,4},{4,0},{8,12},{12,8},{16,20},{20,16},{24,28},{28,24},{32,36},... | collective-permute-start | bytes 737288 | tf_op jit(solution)/shard_map/ppermute | solution.py:582
  18.7 6.3 %collective-permute-start.78 = (f32[3,160,128]{2,1,0:T(8,128)}, f32[3,160,128]{2,1,0:T(8,128)S(1)}, u32[]{:S(2)}, u32[]{:S(2)}) collective-permute-start(f32[3,160,128]{2,1,0:T(8,128)} %get-tuple-element.543), channel_id=1, source_target_pairs={{0,124},{4,8},{8,4},{12,16},{16,12},{20,24},{24,20},{28,32},{32,28... | collective-permute-start | bytes 737288 | tf_op jit(solution)/shard_map/ppermute | solution.py:583
  24.9 1.2 %slice.3 = s32[1]{0:T(128)} slice(s32[4096]{0:T(1024)} %partner.1), slice={[0:1]} | slice | bytes 8 | tf_op jit(solution)/shard_map/slice | solution.py:557
  27.2 21.3 %conditional.7 = (f32[8,160,128]{2,1,0:T(8,128)}, f32[8,160,128]{2,1,0:T(8,128)}, f32[26,160,128]{2,1,0:T(8,128)}) conditional(s32[]{:T(128)} %clamp.3, (f32[8,160,128]{2,1,0:T(8,128)}, f32[2,75,32,128]{3,2,1,0:T(8,128)S(1)}, f32[2,75,32,128]{3,2,1,0:T(8,128)}, f32[2,75,32,128]{3,2,1,0:T(8,128)}, ...), branch_computations={%region_0.0_spmd, %region_1.2_spmd, %region_2.0_spmd, %region_3.0_... | conditional | flops 200000000 | bytes 21242984 | solution.py:600
  27.4 1.9 %collective-permute-start.34 = (f32[8,160,128]{2,1,0:T(8,128)}, f32[8,160,128]{2,1,0:T(8,128)}, u32[]{:S(2)}, u32[]{:S(2)}) collective-permute-start(f32[8,160,128]{2,1,0:T(8,128)} %get-tuple-element.445), channel_id=1, source_target_pairs={{3,71},{7,67},{11,63},{15,59},{19,55},{23,51},{27,47},{31,43},{35,... | collective-permute-start | bytes 1966088 | tf_op jit(solution)/shard_map/cond/branch_17_fun/ppermute | solution.py:586
  29.4 3.0 %collective-permute-start.35 = (f32[8,160,128]{2,1,0:T(8,128)}, f32[8,160,128]{2,1,0:T(8,128)}, u32[]{:S(2)}, u32[]{:S(2)}) collective-permute-start(f32[8,160,128]{2,1,0:T(8,128)} %get-tuple-element.445), channel_id=1, source_target_pairs={{3,67},{7,63},{11,59},{15,55},{19,51},{23,47},{27,43},{31,39},{35,... | collective-permute-start | bytes 1966088 | tf_op jit(solution)/shard_map/cond/branch_17_fun/ppermute | solution.py:587
  32.4 15.0 %inner.49 = f32[26,160,128]{2,1,0:T(8,128)} custom-call(f32[2,75,32,128]{3,2,1,0:T(8,128)S(1)} %get-tuple-element.446.field, f32[2,75,32,128]{3,2,1,0:T(8,128)} %get-tuple-element.447.diff_i, f32[2,75,32,128]{3,2,1,0:T(8,128)} %get-tuple-element.448.diff_j, s32[75,32,128]{2,1,0:T(8,128)} %get-tuple-element.449.land), custom_call_target="tpu_custom_call" | custom-call | flops 200000000 | bytes 16000000 | tf_op jit(solution)/shard_map/cond/branch_17_fun/inner/pallas_call | solution.py:588
  47.4 1.1 %collective-permute-done.34 = f32[8,160,128]{2,1,0:T(8,128)} collective-permute-done((f32[8,160,128]{2,1,0:T(8,128)}, f32[8,160,128]{2,1,0:T(8,128)}, u32[]{:S(2)}, u32[]{:S(2)}) %collective-permute-start.34) | collective-permute-done | bytes 655392 | tf_op jit(solution)/shard_map/cond/branch_17_fun/ppermute | solution.py:586
  48.5 0.0 collective-permute-done.35
  48.5 0.0 collective-permute-done.77.recv_e
  48.5 0.0 copy-start.2
  48.5 0.0 collective-permute-done.78.recv_o
  48.5 0.0 copy-start.3
  48.6 0.7 copy-done.2
  49.2 0.1 copy-done.3
  49.3 19.7 %finish.1 = f32[2,75,32,128]{3,2,1,0:T(8,128)} custom-call(s32[4096]{0:T(1024)} %partner.1, f32[2,75,32,128]{3,2,1,0:T(8,128)S(1)} %copy-done, f32[2,75,32,128]{3,2,1,0:T(8,128)} %diff_i.5, f32[2,75,32,128]{3,2,1,0:T(8,128)} %diff_j.5, s32[75,32,128]{2,1,0:T(8,128)} %land.5, f32[26,160,128]{2,1,0:T(8,128)} %get-tuple-element.535.inner, ...), custom_call_target="tpu_custom_call" | custom-call | tf_op jit(solution)/shard_map/finish/pallas_call | solution.py:603
  (1 shorter events, 0.0 us)
Async XLA Ops:
  0.0 5.3 %copy-start = (f32[2,75,32,128]{3,2,1,0:T(8,128)S(1)}, f32[2,75,32,128]{3,2,1,0:T(8,128)}, u32[]{:S(2)}) copy-start(f32[2,75,32,128]{3,2,1,0:T(8,128)} %field.5) | copy-start | bytes 7372804
  0.0 5.3 %copy-start.1 = (s32[75,32,128]{2,1,0:T(8,128)S(1)}, s32[75,32,128]{2,1,0:T(8,128)}, u32[]{:S(2)}) copy-start(s32[75,32,128]{2,1,0:T(8,128)} %land.5) | copy-start | bytes 3686404
  3.0 11.0 %collective-permute-start.75 = (f32[8,160,128]{2,1,0:T(8,128)}, f32[8,160,128]{2,1,0:T(8,128)}, u32[]{:S(2)}, u32[]{:S(2)}) collective-permute-start(f32[8,160,128]{2,1,0:T(8,128)} %get-tuple-element.537), channel_id=1, source_target_pairs={{0,1},{1,0},{2,3},{3,2},{4,5},{5,4},{6,7},{7,6},{8,9},{9,8},{10,11... | collective-permute-start | bytes 1966088 | tf_op jit(solution)/shard_map/ppermute | solution.py:573
  3.8 10.2 %collective-permute-start.76 = (f32[8,160,128]{2,1,0:T(8,128)}, f32[8,160,128]{2,1,0:T(8,128)}, u32[]{:S(2)}, u32[]{:S(2)}) collective-permute-start(f32[8,160,128]{2,1,0:T(8,128)} %get-tuple-element.534), channel_id=1, source_target_pairs={{1,2},{2,1},{5,6},{6,5},{9,10},{10,9},{13,14},{14,13},{17,18},{18,... | collective-permute-start | bytes 1966088 | tf_op jit(solution)/shard_map/ppermute | solution.py:574
  17.0 31.5 %collective-permute-start.77 = (f32[3,160,128]{2,1,0:T(8,128)}, f32[3,160,128]{2,1,0:T(8,128)S(1)}, u32[]{:S(2)}, u32[]{:S(2)}) collective-permute-start(f32[3,160,128]{2,1,0:T(8,128)} %get-tuple-element.542), channel_id=1, source_target_pairs={{0,4},{4,0},{8,12},{12,8},{16,20},{20,16},{24,28},{28,24},{32,36},... | collective-permute-start | bytes 737288 | tf_op jit(solution)/shard_map/ppermute | solution.py:582
  18.7 29.9 %collective-permute-start.78 = (f32[3,160,128]{2,1,0:T(8,128)}, f32[3,160,128]{2,1,0:T(8,128)S(1)}, u32[]{:S(2)}, u32[]{:S(2)}) collective-permute-start(f32[3,160,128]{2,1,0:T(8,128)} %get-tuple-element.543), channel_id=1, source_target_pairs={{0,124},{4,8},{8,4},{12,16},{16,12},{20,24},{24,20},{28,32},{32,28... | collective-permute-start | bytes 737288 | tf_op jit(solution)/shard_map/ppermute | solution.py:583
  27.4 21.1 %collective-permute-start.34 = (f32[8,160,128]{2,1,0:T(8,128)}, f32[8,160,128]{2,1,0:T(8,128)}, u32[]{:S(2)}, u32[]{:S(2)}) collective-permute-start(f32[8,160,128]{2,1,0:T(8,128)} %get-tuple-element.445), channel_id=1, source_target_pairs={{3,71},{7,67},{11,63},{15,59},{19,55},{23,51},{27,47},{31,43},{35,... | collective-permute-start | bytes 1966088 | tf_op jit(solution)/shard_map/cond/branch_17_fun/ppermute | solution.py:586
  29.4 19.1 %collective-permute-start.35 = (f32[8,160,128]{2,1,0:T(8,128)}, f32[8,160,128]{2,1,0:T(8,128)}, u32[]{:S(2)}, u32[]{:S(2)}) collective-permute-start(f32[8,160,128]{2,1,0:T(8,128)} %get-tuple-element.445), channel_id=1, source_target_pairs={{3,67},{7,63},{11,59},{15,55},{19,51},{23,47},{27,43},{31,39},{35,... | collective-permute-start | bytes 1966088 | tf_op jit(solution)/shard_map/cond/branch_17_fun/ppermute | solution.py:587
  48.5 0.7 %copy-start.2 = (f32[3,160,128]{2,1,0:T(8,128)}, f32[3,160,128]{2,1,0:T(8,128)S(1)}, u32[]{:S(2)}) copy-start(f32[3,160,128]{2,1,0:T(8,128)S(1)} %collective-permute-done.77.recv_e) | copy-start | bytes 737284
  48.5 0.8 %copy-start.3 = (f32[3,160,128]{2,1,0:T(8,128)}, f32[3,160,128]{2,1,0:T(8,128)S(1)}, u32[]{:S(2)}) copy-start(f32[3,160,128]{2,1,0:T(8,128)S(1)} %collective-permute-done.78.recv_o) | copy-start | bytes 737284

commit v3 on v2

--- a/solution.py
+++ b/solution.py
@@ -80,39 +80,50 @@
     return (lax.axis_index("ia") & 1) == 1, (lax.axis_index("ja") & 1) == 1
 
 
+PARTS = [(0, 0, L), (1, 0, L)]
+LAND_PARTS = [(0, L)]
+
+
 def start_rows(raw, kept, sems, spans):
-    field, diff_i, diff_j, land = raw
-    f, di, dj, ls = kept
-    for v in range(V):
-        at = pl.ds(v * SLOTS, L)
+    land, ls = raw[3], kept[3]
+    for c, (v, level, depth) in enumerate(PARTS):
+        source = pl.ds(level, depth)
+        at = pl.ds(v * SLOTS + level, depth)
         for low, count in spans:
 
             def row(r, carry):
-                pltpu.make_async_copy(field.at[v, :, r], f.at[r, at], sems.at[v]).start()
-                pltpu.make_async_copy(diff_i.at[v, :, r], di.at[r, at], sems.at[2 + v]).start()
-                pltpu.make_async_copy(diff_j.at[v, :, r], dj.at[r, at], sems.at[4 + v]).start()
+                for j in range(3):
+                    pltpu.make_async_copy(raw[j].at[v, source, r], kept[j].at[r, at], sems.at[3 * c + j]).start()
                 return carry
 
             lax.fori_loop(low, low + count, row, 0)
 
 
-def start_land(land, ls, sem, spans):
-    for low, count in spans:
-
-        def row(r, carry):
-            pltpu.make_async_copy(land.at[:, r], ls.at[r, pl.ds(0, L)], sem).start()
-            return carry
-
-        lax.fori_loop(low, low + count, row, 0)
+def start_land(land, ls, sems, spans):
+    for c, (level, depth) in enumerate(LAND_PARTS):
+        at = pl.ds(level, depth)
+        for low, count in spans:
+
+            def row(r, carry):
+                pltpu.make_async_copy(land.at[at, r], ls.at[r, at], sems.at[9 + c]).start()
+                return carry
+
+            lax.fori_loop(low, low + count, row, 0)
 
 
 def wait_for(ref, sem):
     pltpu.make_async_copy(ref, ref, sem).wait()
 
 
-def wait_rows(kept, sems, v, count):
+def wait_rows(kept, sems, c, count):
+    v, level, depth = PARTS[c]
     for j in range(3):
-        wait_for(kept[j].at[pl.ds(0, count), pl.ds(v * SLOTS, L)], sems.at[2 * j + v])
+        wait_for(kept[j].at[pl.ds(0, count), pl.ds(v * SLOTS + level, depth)], sems.at[3 * c + j])
+
+
+def wait_land(ls, sems, c, count):
+    level, depth = LAND_PARTS[c]
+    wait_for(ls.at[pl.ds(0, count), pl.ds(level, depth)], sems.at[9 + c])
 
 
 def root(x):
@@ -136,18 +147,20 @@
     pltpu.VMEM((R, DEPTH, C), jnp.float32),
     pltpu.VMEM((R, DEPTH, C), jnp.float32),
     pltpu.VMEM((R, SLOTS, C), jnp.int32),
-    pltpu.SemaphoreType.DMA((7,)),
+    pltpu.SemaphoreType.DMA((11,)),
 ]
 ALL_ROWS = [(0, R)]
 
 
-def tiles(kept, sems, count, tall, tile):
+def tiles(kept, sems, count, tall, tile, land_rows=0):
     def body(t, carry):
-        for v in range(V):
-
-            @pl.when(t == v * (SLOTS // tall))
+        for c, (v, level, depth) in enumerate(PARTS):
+
+            @pl.when(t == (v * SLOTS + level) // tall)
             def _():
-                wait_rows(kept, sems, v, count)
+                if land_rows and c < len(LAND_PARTS):
+                    wait_land(kept[3], sems, c, land_rows)
+                wait_rows(kept, sems, c, count)
 
         tile(t)
         return carry
@@ -160,21 +173,21 @@
 OUTER_ROWS = [(0, 3), (R - 3, 3)]
 
 
-def wait_land(ls, sem, count):
-    wait_for(ls.at[pl.ds(0, count), pl.ds(0, L)], sem)
-
-
 ROWS_TALL = 40
 COLUMNS_TALL = 40
 
 
-def rows_kernel(field, diff_i, diff_j, land, send_a, send_b, send_x, f, di, dj, ls, sems):
+def rows_kernel(
+    field, diff_i, diff_j, land, partner, send_a, send_b, send_x, block, special, centre, centre_sem,
+    f, di, dj, ls, sems,
+):
+    centre_copy = pltpu.make_async_copy(partner.at[pl.ds(0, C)], centre, centre_sem)
+    centre_copy.start()
     _, j_odd = parities()
     kept = (f, di, dj, ls)
-    start_land(land, ls, sems.at[6], OUTER_ROWS)
+    start_land(land, ls, sems, OUTER_ROWS)
     start_rows((field, diff_i, diff_j, land), kept, sems, OUTER_ROWS)
     slot = slot_of(lanes(ROWS_TALL))
-    wait_land(ls, sems.at[6], 6)
 
     def tile(t):
         rows = span(ROWS_TALL, t)
@@ -187,21 +200,23 @@
             third = jnp.where(slot == g, roll(top, 16 * g), third)
         send_x[rows, :] = third
 
-    tiles(kept, sems, 6, ROWS_TALL, tile)
+    tiles(kept, sems, 6, ROWS_TALL, tile, 6)
+    centre_copy.wait()
+    block[0] = centre[0] >> 7
+    shift = centre[0] & (C - 1)
+    special[0] = jnp.where((shift <= 1) | (shift >= C - 3), 1, 0)
 
 
 def columns_kernel(
-    field, diff_i, diff_j, land, columns_e, columns_o, strips, f, di, dj, ls, sems
+    field, diff_i, diff_j, land, columns_e, columns_o, strips, packed_rows, out_sem, f, di, dj, ls, sems
 ):
     i_odd, _ = parities()
     kept = (f, di, dj, ls)
-    start_land(land, ls, sems.at[6], ALL_ROWS)
+    start_land(land, ls, sems, ALL_ROWS)
     start_rows((field, diff_i, diff_j, land), kept, sems, ALL_ROWS)
     lane = lanes(COLUMNS_TALL)
     slot = slot_of(lane)
     in_slot = lane & 15
-    wait_land(ls, sems.at[6], R)
-
     def tile(t):
         rows = span(COLUMNS_TALL, t)
         packed = [[jnp.zeros((COLUMNS_TALL, C), jnp.float32) for _ in range(PLANES)] for _ in range(3)]
@@ -213,14 +228,16 @@
         for a in range(3):
             left, right = packed[a][0], packed[a][0]
             for p in range(PLANES):
-                strips[a, p, rows, :] = packed[a][p]
+                packed_rows[a, p, rows, :] = packed[a][p]
                 if p:
                     left = jnp.where(in_slot >= 3 * p, roll(packed[a][p], 3 * p), left)
                     right = jnp.where(in_slot < 16 - 3 * p, roll(packed[a][p], -3 * p), right)
             columns_e[a, rows, :] = jnp.where(i_odd, left, right)
             columns_o[a, rows, :] = jnp.where(i_odd, right, left)
-
-    tiles(kept, sems, R, COLUMNS_TALL, tile)
+        pltpu.make_async_copy(packed_rows.at[:, :, rows], strips.at[:, :, rows], out_sem).start()
+
+    tiles(kept, sems, R, COLUMNS_TALL, tile, R)
+    wait_for(packed_rows, out_sem)
 
 
 WIDE = 80
@@ -313,36 +330,40 @@
 INNER_TALL = 8
 
 
-def inner_kernel(field, diff_i, diff_j, land, out, f, di, dj, ls, sems):
+def inner_kernel(field, diff_i, diff_j, land, out, done, out_sem, f, di, dj, ls, sems):
     kept = (f, di, dj, ls)
-    start_land(land, ls, sems.at[6], ALL_ROWS)
+    start_land(land, ls, sems, ALL_ROWS)
     start_rows((field, diff_i, diff_j, land), kept, sems, ALL_ROWS)
     not_last = jnp.where(lanes(INNER_TALL) == C - 1, 0.0, 1.0)
-    wait_for(ls.at[:, pl.ds(0, L)], sems.at[6])
 
     def tile(t):
+        rows = span(INNER_TALL, t)
+
         def emit(r, value):
-            out[r - 3, span(INNER_TALL, t), :] = value
+            done[r - 3, rows, :] = value
 
         stream(3, R - 3, lambda r: cell(kept, INNER_TALL, t, r), emit, not_last)
-
-    tiles(kept, sems, R, INNER_TALL, tile)
-
-
-STRIP_TALL = 40
-EDGE_TALL = 40
+        pltpu.make_async_copy(done.at[:, rows], out.at[:, rows], out_sem).start()
+
+    tiles(kept, sems, R, INNER_TALL, tile, R)
+    wait_for(done, out_sem)
+
+
+STRIP_TALL = 160
+EDGE_TALL = 80
 
 
 def finish_kernel(
-    partner, field, diff_i, diff_j, land, inner, vertical, strips,
+    field, diff_i, diff_j, land, inner, vertical, partner, strips,
     recv_a, recv_b, near, far, recv_e, recv_o, recv_x,
-    out, north, south, north_halo, east, west, fold, own_strips, fixed, diffused, mixed, square, weights,
+    out, north, south, north_halo, east, west, fold, own_strips, fixed, diffused, mixed, square, weights, centre, centre_sem,
     f, di, dj, ls, sems, got, out_sem,
 ):
     i_odd, j_odd = parities()
     at_top = lax.axis_index("ja") == 3
     at_bottom = lax.axis_index("ja") == 0
-    shift = partner[0] & (C - 1)
+    centre_copy = pltpu.make_async_copy(partner.at[pl.ds(0, C)], centre, centre_sem)
+    centre_copy.start()
     kept = (f, di, dj, ls)
 
     def choose(flag, first, second, to, sem):
@@ -370,7 +391,7 @@
     strips_copy = pltpu.make_async_copy(strips, own_strips, got.at[6])
     strips_copy.start()
     start_rows((field, diff_i, diff_j, land), kept, sems, EDGE_ROWS)
-    start_land(land, ls, sems.at[6], ALL_ROWS)
+    start_land(land, ls, sems, ALL_ROWS)
     inner_copy = pltpu.make_async_copy(inner, diffused.at[pl.ds(3, R - 6)], got.at[5])
     inner_copy.start()
 
@@ -387,6 +408,9 @@
 
     for j, ref in enumerate((east, west, north, south)):
         wait_for(ref, got.at[j])
+
+    centre_copy.wait()
+    shift = centre[0] & (C - 1)
 
     @pl.when(at_top)
     def _():
@@ -450,7 +474,8 @@
     lax.fori_loop(0, 2 * (DEPTH // STRIP_TALL), strip_tile, 0)
 
     not_last = jnp.where(lanes(EDGE_TALL) == C - 1, 0.0, 1.0)
-    wait_land(ls, sems.at[6], R)
+    for c in range(len(LAND_PARTS)):
+        wait_land(ls, sems, c, R)
 
     def edge_tile(t, low):
         rows = span(EDGE_TALL, t)
@@ -525,21 +550,24 @@
     def cost(flops, size):
         return pl.CostEstimate(flops=flops, bytes_accessed=size, transcendentals=0)
 
-    send_a, send_b, send_x = pl.pallas_call(
+    smem = pl.BlockSpec(memory_space=pltpu.SMEM)
+    number = jax.ShapeDtypeStruct((1,), jnp.int32)
+    send_a, send_b, send_x, block, special = pl.pallas_call(
         rows_kernel,
-        in_specs=[hbm] * 4,
-        out_specs=[vmem] * 3,
-        out_shape=[planes(8), planes(8), planes()],
-        scratch_shapes=RAW_SCRATCH,
+        in_specs=[hbm] * 5,
+        out_specs=[vmem] * 3 + [smem] * 2,
+        out_shape=[planes(8), planes(8), planes(), number, number],
+        scratch_shapes=[pltpu.SMEM((C,), jnp.int32), pltpu.SemaphoreType.DMA] + RAW_SCRATCH,
         compiler_params=big,
         name="pack_rows",
-    )(*raw)
+    )(*raw, partner)
+    block, special = block.reshape(()), special.reshape(())
     columns_e, columns_o, strips = pl.pallas_call(
         columns_kernel,
         in_specs=[hbm] * 4,
-        out_specs=[vmem] * 3,
+        out_specs=[vmem] * 2 + [hbm],
         out_shape=[planes(3), planes(3), planes(3, PLANES)],
-        scratch_shapes=RAW_SCRATCH,
+        scratch_shapes=[scratch(3, PLANES), pltpu.SemaphoreType.DMA] + RAW_SCRATCH,
         compiler_params=big,
         cost_estimate=cost(10**8, 16 * 10**6),
         name="pack_columns",
@@ -554,21 +582,18 @@
     def fold(q):
         return [(t * 4 + 3, ((q - t) % count) * 4 + 3) for t in range(count)]
 
-    centre = partner[0]
-    block, shift = lax.shift_right_logical(centre, 7), centre & (C - 1)
-
     def mirror(x, q):
         return lax.ppermute(x, both, fold(q))
 
     def third_block(x):
-        turn = jnp.where(shift <= 1, block - 2, block + 1)
+        turn = jnp.where(partner[0] & (C - 1) <= 1, block - 2, block + 1)
         x = mirror(x, 0)
         for bit in range((count - 1).bit_length()):
             rotate = functools.partial(lambda y, step: mirror(mirror(y, 0), step), step=2**bit)
             x = lax.cond((turn >> bit) & 1 == 1, rotate, lambda y: y, x)
         return x
 
-    recv_x = lax.cond((shift <= 1) | (shift >= C - 3), third_block, lambda x: x, send_x)
+    recv_x = lax.cond(special == 1, third_block, lambda x: x, send_x)
 
     recv_a = lax.ppermute(send_a, "ja", rows_a)
     recv_b = lax.ppermute(send_b, "ja", rows_b)
@@ -588,9 +613,9 @@
         inner = pl.pallas_call(
             inner_kernel,
             in_specs=[hbm] * 4,
-            out_specs=vmem,
+            out_specs=hbm,
             out_shape=planes(R - 6),
-            scratch_shapes=RAW_SCRATCH,
+            scratch_shapes=[scratch(R - 6), pltpu.SemaphoreType.DMA] + RAW_SCRATCH,
             compiler_params=big,
             cost_estimate=cost(2 * 10**8, 16 * 10**6),
             name="inner",
@@ -602,18 +627,19 @@
     )
     return pl.pallas_call(
         finish_kernel,
-        in_specs=[pl.BlockSpec(memory_space=pltpu.SMEM)] + [hbm] * 5 + [vmem] + [hbm] * 7 + [vmem],
+        in_specs=[hbm] * 5 + [vmem] + [hbm] * 8 + [vmem],
         out_specs=hbm,
         out_shape=jax.ShapeDtypeStruct((V, L, R, C), jnp.float32),
         scratch_shapes=[
             scratch(8), scratch(8), scratch(), scratch(3), scratch(3), scratch(8),
             scratch(3, PLANES), scratch(2, PLANES), scratch(R), scratch(R),
             pltpu.VMEM((V, SLOTS, C), jnp.float32), pltpu.VMEM((V, SLOTS, 2 * C), jnp.bfloat16),
+            pltpu.SMEM((C,), jnp.int32), pltpu.SemaphoreType.DMA,
         ] + RAW_SCRATCH + [pltpu.SemaphoreType.DMA((7,)), pltpu.SemaphoreType.DMA((V,))],
         compiler_params=big,
         name="finish",
     )(
-        partner, *raw, inner, jnp.swapaxes(vertical, 0, 1), strips,
+        *raw, inner, jnp.swapaxes(vertical, 0, 1), partner, strips,
         recv_a, recv_b, near, far, recv_e, recv_o, recv_x,
     )
 

time: 70.4 us -> 69.2 us (0.983)
  the two profiles are of different devices: /device:TPU:3 before, /device:TPU:27 now
where the time goes in v3:
time: 69.2 us; the launch traced here: 68.7 us
  Pallas kernels  48 us (69%)
  starting transfers between devices  17.9 us (26%)
  between operations  1.47 us (2%)
  local copies, waits for them, and re-layouts  0.78 us (1%)
    pallas_call x1, Pallas kernels, body(): pl.pallas_call(finish_kernel, in_specs=[hbm] * 5 + [vmem] + [hbm] * 8 + [...  18.5 us
    pallas_call x1, Pallas kernels, fold_and_inner(): pl.pallas_call(inner_kernel, in_specs=[hbm] * 4, out_specs=hbm, out_shape...  14.4 us
    pallas_call x1, Pallas kernels, body(): pl.pallas_call(columns_kernel, in_specs=[hbm] * 4, out_specs=[vmem] * 2 +...  8.93 us
    ppermute x1, starting transfers between devices, fold_and_inner(): far = lax.ppermute(send_b, both, fold((q - 1) % count))  7.94 us
    ppermute x1, starting transfers between devices, fold_and_inner(): near = lax.ppermute(send_b, both, fold(q))  3.64 us
    pallas_call x1, Pallas kernels, body(): pl.pallas_call(rows_kernel, in_specs=[hbm] * 5, out_specs=[vmem] * 3 + [s...  3.15 us
    pallas_call x1, Pallas kernels, body(): pl.pallas_call(ghost_kernel, in_specs=[vmem] * 4, out_specs=[vmem] * 2, o...  3.03 us
    ppermute x1, starting transfers between devices, body(): recv_o = lax.ppermute(send_o, 'ia', odd)  2.42 us
  transfers between devices with their start and end apart: 6, of which 0 were waited for; matrix products, arithmetic and copies ran while one was open for 0% of the time, Pallas kernels for 34%

profile of v3, /device:TPU:27, one launch (start us, length us, event | category | flops | bytes accessed | tf_op | source)
XLA Modules:
  0.0 68.7 jit_solution(7875785402712741834)
XLA Ops:
  0.0 0.0 copy-start
  0.0 0.0 copy-start.1
  0.0 3.2 %pack_rows.1 = (f32[8,160,128]{2,1,0:T(8,128)}, f32[8,160,128]{2,1,0:T(8,128)}, f32[160,128]{1,0:T(8,128)S(1)}, s32[1]{0:T(128)}, s32[1]{0:T(128)}) custom-call(f32[2,75,32,128]{3,2,1,0:T(8,128)} %field.5, f32[2,75,32,128]{3,2,1,0:T(8,128)} %diff_i.5, f32[2,75,32,128]{3,2,1,0:T(8,128)} %diff_j.5, s32[75,32,128]{2,1,0:T(8,128)} %land.5, s32[4096]{0:T(1024)} %partner.3), custom_call_target="tpu_custom_call" | custom-call | tf_op jit(solution)/shard_map/pack_rows/pallas_call | solution.py:555
  3.2 0.8 %collective-permute-start.75 = (f32[8,160,128]{2,1,0:T(8,128)}, f32[8,160,128]{2,1,0:T(8,128)}, u32[]{:S(2)}, u32[]{:S(2)}) collective-permute-start(f32[8,160,128]{2,1,0:T(8,128)} %get-tuple-element.540), channel_id=1, source_target_pairs={{0,1},{1,0},{2,3},{3,2},{4,5},{5,4},{6,7},{7,6},{8,9},{9,8},{10,11... | collective-permute-start | bytes 1966088 | tf_op jit(solution)/shard_map/ppermute | solution.py:598
  3.9 1.5 %collective-permute-start.76 = (f32[8,160,128]{2,1,0:T(8,128)}, f32[8,160,128]{2,1,0:T(8,128)}, u32[]{:S(2)}, u32[]{:S(2)}) collective-permute-start(f32[8,160,128]{2,1,0:T(8,128)} %get-tuple-element.537), channel_id=1, source_target_pairs={{1,2},{2,1},{5,6},{6,5},{9,10},{10,9},{13,14},{14,13},{17,18},{18,... | collective-permute-start | bytes 1966088 | tf_op jit(solution)/shard_map/ppermute | solution.py:599
  5.4 0.0 copy-done
  5.4 0.0 copy-done.1
  5.4 8.9 %pack_columns.1 = (f32[3,160,128]{2,1,0:T(8,128)}, f32[3,160,128]{2,1,0:T(8,128)}, f32[3,5,160,128]{3,2,1,0:T(8,128)}) custom-call(f32[2,75,32,128]{3,2,1,0:T(8,128)S(1)} %copy-done, f32[2,75,32,128]{3,2,1,0:T(8,128)} %diff_i.5, f32[2,75,32,128]{3,2,1,0:T(8,128)} %diff_j.5, s32[75,32,128]{2,1,0:T(8,128)S(1)} %copy-done.1), custom_call_target="tpu_custom_call" | custom-call | flops 100000000 | bytes 16000000 | tf_op jit(solution)/shard_map/pack_columns/pallas_call | solution.py:565
  14.4 0.0 collective-permute-done.75.recv_a
  14.4 0.0 collective-permute-done.76.recv_b
  14.4 3.0 %pack_ghost_columns.1 = (f32[3,160,128]{2,1,0:T(8,128)}, f32[3,160,128]{2,1,0:T(8,128)}) custom-call(f32[3,160,128]{2,1,0:T(8,128)} %get-tuple-element.543.columns_e, f32[3,160,128]{2,1,0:T(8,128)} %get-tuple-element.544.columns_o, f32[8,160,128]{2,1,0:T(8,128)} %collective-permute-done.75.recv_a, f32[8,160,128]{2,1,0:T(8,128)} %collective-permute-done.76.recv_b), custom_call_target="tpu_custom_call" | custom-call | tf_op jit(solution)/shard_map/pack_ghost_columns/pallas_call | solution.py:600
  17.4 1.6 %collective-permute-start.77 = (f32[3,160,128]{2,1,0:T(8,128)}, f32[3,160,128]{2,1,0:T(8,128)S(1)}, u32[]{:S(2)}, u32[]{:S(2)}) collective-permute-start(f32[3,160,128]{2,1,0:T(8,128)} %get-tuple-element.545), channel_id=1, source_target_pairs={{0,4},{4,0},{8,12},{12,8},{16,20},{20,16},{24,28},{28,24},{32,36},... | collective-permute-start | bytes 737288 | tf_op jit(solution)/shard_map/ppermute | solution.py:607
  19.1 2.4 %collective-permute-start.78 = (f32[3,160,128]{2,1,0:T(8,128)}, f32[3,160,128]{2,1,0:T(8,128)S(1)}, u32[]{:S(2)}, u32[]{:S(2)}) collective-permute-start(f32[3,160,128]{2,1,0:T(8,128)} %get-tuple-element.546), channel_id=1, source_target_pairs={{0,124},{4,8},{8,4},{12,16},{16,12},{20,24},{24,20},{28,32},{32,28... | collective-permute-start | bytes 737288 | tf_op jit(solution)/shard_map/ppermute | solution.py:608
  22.7 0.0 copy-start.4
  22.7 26.5 %conditional.7 = (f32[8,160,128]{2,1,0:T(8,128)}, f32[8,160,128]{2,1,0:T(8,128)}, f32[26,160,128]{2,1,0:T(8,128)}) conditional(s32[]{:T(128)} %clamp.3, (f32[8,160,128]{2,1,0:T(8,128)}, f32[2,75,32,128]{3,2,1,0:T(8,128)S(1)}, f32[2,75,32,128]{3,2,1,0:T(8,128)}, f32[2,75,32,128]{3,2,1,0:T(8,128)}, ...), branch_computations={%region_0.0_spmd, %region_1.2_spmd, %region_2.0_spmd, %region_3.0_... | conditional | flops 200000000 | bytes 21242984 | solution.py:625
  22.7 3.6 %collective-permute-start.8 = (f32[8,160,128]{2,1,0:T(8,128)}, f32[8,160,128]{2,1,0:T(8,128)}, u32[]{:S(2)}, u32[]{:S(2)}) collective-permute-start(f32[8,160,128]{2,1,0:T(8,128)} %get-tuple-element.380), channel_id=1, source_target_pairs={{3,19},{7,15},{11,11},{15,7},{19,3},{23,127},{27,123},{31,119},{35... | collective-permute-start | bytes 1966088 | tf_op jit(solution)/shard_map/cond/branch_4_fun/ppermute | solution.py:611
  26.4 7.9 %collective-permute-start.9 = (f32[8,160,128]{2,1,0:T(8,128)}, f32[8,160,128]{2,1,0:T(8,128)}, u32[]{:S(2)}, u32[]{:S(2)}) collective-permute-start(f32[8,160,128]{2,1,0:T(8,128)} %get-tuple-element.380), channel_id=1, source_target_pairs={{3,15},{7,11},{11,7},{15,3},{19,127},{23,123},{27,119},{31,115},{3... | collective-permute-start | bytes 1966088 | tf_op jit(solution)/shard_map/cond/branch_4_fun/ppermute | solution.py:612
  34.3 14.4 %inner.36 = f32[26,160,128]{2,1,0:T(8,128)} custom-call(f32[2,75,32,128]{3,2,1,0:T(8,128)S(1)} %get-tuple-element.381.field, f32[2,75,32,128]{3,2,1,0:T(8,128)} %get-tuple-element.382.diff_i, f32[2,75,32,128]{3,2,1,0:T(8,128)} %get-tuple-element.383.diff_j, s32[75,32,128]{2,1,0:T(8,128)} %get-tuple-element.384.land), custom_call_target="tpu_custom_call" | custom-call | flops 200000000 | bytes 16000000 | tf_op jit(solution)/shard_map/cond/branch_4_fun/inner/pallas_call | solution.py:613
  48.7 0.0 collective-permute-done.8
  48.8 0.0 collective-permute-done.9
  49.2 0.0 copy-done.4
  49.2 0.0 collective-permute-done.77.recv_e
  49.2 0.0 copy-start.2
  49.2 0.0 collective-permute-done.78.recv_o
  49.3 0.0 copy-start.3
  49.3 0.7 copy-done.2
  49.9 0.1 copy-done.3
  50.0 18.5 %finish.1 = f32[2,75,32,128]{3,2,1,0:T(8,128)} custom-call(f32[2,75,32,128]{3,2,1,0:T(8,128)S(1)} %copy-done, f32[2,75,32,128]{3,2,1,0:T(8,128)} %diff_i.5, f32[2,75,32,128]{3,2,1,0:T(8,128)} %diff_j.5, s32[75,32,128]{2,1,0:T(8,128)} %land.5, f32[26,160,128]{2,1,0:T(8,128)} %get-tuple-element.538.inner, f32[75,2,75]{2,1,0:T(2,128)} %bitcast.4, ...), custom_call_target="tpu_custom_call" | custom-call | tf_op jit(solution)/shard_map/finish/pallas_call | solution.py:628
  (1 shorter events, 0.0 us)
Async XLA Ops:
  0.0 5.4 %copy-start = (f32[2,75,32,128]{3,2,1,0:T(8,128)S(1)}, f32[2,75,32,128]{3,2,1,0:T(8,128)}, u32[]{:S(2)}) copy-start(f32[2,75,32,128]{3,2,1,0:T(8,128)} %field.5) | copy-start | bytes 7372804
  0.0 5.4 %copy-start.1 = (s32[75,32,128]{2,1,0:T(8,128)S(1)}, s32[75,32,128]{2,1,0:T(8,128)}, u32[]{:S(2)}) copy-start(s32[75,32,128]{2,1,0:T(8,128)} %land.5) | copy-start | bytes 3686404
  3.2 11.2 %collective-permute-start.75 = (f32[8,160,128]{2,1,0:T(8,128)}, f32[8,160,128]{2,1,0:T(8,128)}, u32[]{:S(2)}, u32[]{:S(2)}) collective-permute-start(f32[8,160,128]{2,1,0:T(8,128)} %get-tuple-element.540), channel_id=1, source_target_pairs={{0,1},{1,0},{2,3},{3,2},{4,5},{5,4},{6,7},{7,6},{8,9},{9,8},{10,11... | collective-permute-start | bytes 1966088 | tf_op jit(solution)/shard_map/ppermute | solution.py:598
  3.9 10.5 %collective-permute-start.76 = (f32[8,160,128]{2,1,0:T(8,128)}, f32[8,160,128]{2,1,0:T(8,128)}, u32[]{:S(2)}, u32[]{:S(2)}) collective-permute-start(f32[8,160,128]{2,1,0:T(8,128)} %get-tuple-element.537), channel_id=1, source_target_pairs={{1,2},{2,1},{5,6},{6,5},{9,10},{10,9},{13,14},{14,13},{17,18},{18,... | collective-permute-start | bytes 1966088 | tf_op jit(solution)/shard_map/ppermute | solution.py:599
  17.4 31.8 %collective-permute-start.77 = (f32[3,160,128]{2,1,0:T(8,128)}, f32[3,160,128]{2,1,0:T(8,128)S(1)}, u32[]{:S(2)}, u32[]{:S(2)}) collective-permute-start(f32[3,160,128]{2,1,0:T(8,128)} %get-tuple-element.545), channel_id=1, source_target_pairs={{0,4},{4,0},{8,12},{12,8},{16,20},{20,16},{24,28},{28,24},{32,36},... | collective-permute-start | bytes 737288 | tf_op jit(solution)/shard_map/ppermute | solution.py:607
  19.1 30.2 %collective-permute-start.78 = (f32[3,160,128]{2,1,0:T(8,128)}, f32[3,160,128]{2,1,0:T(8,128)S(1)}, u32[]{:S(2)}, u32[]{:S(2)}) collective-permute-start(f32[3,160,128]{2,1,0:T(8,128)} %get-tuple-element.546), channel_id=1, source_target_pairs={{0,124},{4,8},{8,4},{12,16},{16,12},{20,24},{24,20},{28,32},{32,28... | collective-permute-start | bytes 737288 | tf_op jit(solution)/shard_map/ppermute | solution.py:608
  22.7 26.5 %copy-start.4 = (s32[4096]{0:T(1024)S(1)}, s32[4096]{0:T(1024)}, u32[]{:S(2)}) copy-start(s32[4096]{0:T(1024)} %partner.3) | copy-start | bytes 49156
  22.7 26.0 %collective-permute-start.8 = (f32[8,160,128]{2,1,0:T(8,128)}, f32[8,160,128]{2,1,0:T(8,128)}, u32[]{:S(2)}, u32[]{:S(2)}) collective-permute-start(f32[8,160,128]{2,1,0:T(8,128)} %get-tuple-element.380), channel_id=1, source_target_pairs={{3,19},{7,15},{11,11},{15,7},{19,3},{23,127},{27,123},{31,119},{35... | collective-permute-start | bytes 1966088 | tf_op jit(solution)/shard_map/cond/branch_4_fun/ppermute | solution.py:611
  26.4 22.4 %collective-permute-start.9 = (f32[8,160,128]{2,1,0:T(8,128)}, f32[8,160,128]{2,1,0:T(8,128)}, u32[]{:S(2)}, u32[]{:S(2)}) collective-permute-start(f32[8,160,128]{2,1,0:T(8,128)} %get-tuple-element.380), channel_id=1, source_target_pairs={{3,15},{7,11},{11,7},{15,3},{19,127},{23,123},{27,119},{31,115},{3... | collective-permute-start | bytes 1966088 | tf_op jit(solution)/shard_map/cond/branch_4_fun/ppermute | solution.py:612
  49.2 0.7 %copy-start.2 = (f32[3,160,128]{2,1,0:T(8,128)}, f32[3,160,128]{2,1,0:T(8,128)S(1)}, u32[]{:S(2)}) copy-start(f32[3,160,128]{2,1,0:T(8,128)S(1)} %collective-permute-done.77.recv_e) | copy-start | bytes 737284
  49.3 0.8 %copy-start.3 = (f32[3,160,128]{2,1,0:T(8,128)}, f32[3,160,128]{2,1,0:T(8,128)S(1)}, u32[]{:S(2)}) copy-start(f32[3,160,128]{2,1,0:T(8,128)S(1)} %collective-permute-done.78.recv_o) | copy-start | bytes 737284

commit v4 on v3

--- a/solution.py
+++ b/solution.py
@@ -430,7 +430,7 @@
             north_halo[...] = jnp.where(wide_slot == g, other, north_halo[...])
             return carry
 
-        lax.fori_loop(0, 8, ghost, 0)
+        lax.fori_loop(0, 8, ghost, 0, unroll=2)
 
     @pl.when(at_bottom)
     def _():
@@ -528,7 +528,7 @@
                 pltpu.make_async_copy(mixed.at[r, pl.ds(v * SLOTS, L)], out.at[v, :, r], out_sem.at[v]).start()
             return carry
 
-        lax.fori_loop(0, R // 2, pair_of_rows, 0, unroll=2)
+        lax.fori_loop(0, R // 2, pair_of_rows, 0, unroll=4)
 
     for v in range(V):
         wait_for(mixed.at[:, pl.ds(v * SLOTS, L)], out_sem.at[v])

time: 69.2 us -> 67.1 us (0.970)
  the two profiles are of different devices: /device:TPU:27 before, /device:TPU:3 now
where the time goes in v4:
time: 67.1 us; the launch traced here: 66.9 us
  Pallas kernels  45.5 us (68%)
  starting transfers between devices  18.6 us (28%)
  between operations  1.47 us (2%)
  local copies, waits for them, and re-layouts  0.78 us (1%)
    pallas_call x1, Pallas kernels, body(): pl.pallas_call(finish_kernel, in_specs=[hbm] * 5 + [vmem] + [hbm] * 8 + [...  16.1 us
    pallas_call x1, Pallas kernels, fold_and_inner(): pl.pallas_call(inner_kernel, in_specs=[hbm] * 4, out_specs=hbm, out_shape...  14.3 us
    pallas_call x1, Pallas kernels, body(): pl.pallas_call(columns_kernel, in_specs=[hbm] * 4, out_specs=[vmem] * 2 +...  8.93 us
    ppermute x1, starting transfers between devices, fold_and_inner(): far = lax.ppermute(send_b, both, fold((q - 1) % count))  6.51 us
    ppermute x1, starting transfers between devices, body(): recv_o = lax.ppermute(send_o, 'ia', odd)  6.25 us
    pallas_call x1, Pallas kernels, body(): pl.pallas_call(rows_kernel, in_specs=[hbm] * 5, out_specs=[vmem] * 3 + [s...  3.15 us
    pallas_call x1, Pallas kernels, body(): pl.pallas_call(ghost_kernel, in_specs=[vmem] * 4, out_specs=[vmem] * 2, o...  3.03 us
    ppermute x1, starting transfers between devices, fold_and_inner(): near = lax.ppermute(send_b, both, fold(q))  1.92 us
  transfers between devices with their start and end apart: 6, of which 0 were waited for; matrix products, arithmetic and copies ran while one was open for 0% of the time, Pallas kernels for 35%

profile of v4, /device:TPU:3, one launch (start us, length us, event | category | flops | bytes accessed | tf_op | source)
XLA Modules:
  0.0 66.9 jit_solution(1015218218844938053)
XLA Ops:
  0.0 0.0 copy-start
  0.0 0.0 copy-start.1
  0.0 3.2 %pack_rows.1 = (f32[8,160,128]{2,1,0:T(8,128)}, f32[8,160,128]{2,1,0:T(8,128)}, f32[160,128]{1,0:T(8,128)S(1)}, s32[1]{0:T(128)}, s32[1]{0:T(128)}) custom-call(f32[2,75,32,128]{3,2,1,0:T(8,128)} %field.5, f32[2,75,32,128]{3,2,1,0:T(8,128)} %diff_i.5, f32[2,75,32,128]{3,2,1,0:T(8,128)} %diff_j.5, s32[75,32,128]{2,1,0:T(8,128)} %land.5, s32[4096]{0:T(1024)} %partner.3), custom_call_target="tpu_custom_call" | custom-call | tf_op jit(solution)/shard_map/pack_rows/pallas_call | solution.py:555
  3.2 0.8 %collective-permute-start.75 = (f32[8,160,128]{2,1,0:T(8,128)}, f32[8,160,128]{2,1,0:T(8,128)}, u32[]{:S(2)}, u32[]{:S(2)}) collective-permute-start(f32[8,160,128]{2,1,0:T(8,128)} %get-tuple-element.540), channel_id=1, source_target_pairs={{0,1},{1,0},{2,3},{3,2},{4,5},{5,4},{6,7},{7,6},{8,9},{9,8},{10,11... | collective-permute-start | bytes 1966088 | tf_op jit(solution)/shard_map/ppermute | solution.py:598
  3.9 1.5 %collective-permute-start.76 = (f32[8,160,128]{2,1,0:T(8,128)}, f32[8,160,128]{2,1,0:T(8,128)}, u32[]{:S(2)}, u32[]{:S(2)}) collective-permute-start(f32[8,160,128]{2,1,0:T(8,128)} %get-tuple-element.537), channel_id=1, source_target_pairs={{1,2},{2,1},{5,6},{6,5},{9,10},{10,9},{13,14},{14,13},{17,18},{18,... | collective-permute-start | bytes 1966088 | tf_op jit(solution)/shard_map/ppermute | solution.py:599
  5.4 0.0 copy-done
  5.4 0.0 copy-done.1
  5.4 8.9 %pack_columns.1 = (f32[3,160,128]{2,1,0:T(8,128)}, f32[3,160,128]{2,1,0:T(8,128)}, f32[3,5,160,128]{3,2,1,0:T(8,128)}) custom-call(f32[2,75,32,128]{3,2,1,0:T(8,128)S(1)} %copy-done, f32[2,75,32,128]{3,2,1,0:T(8,128)} %diff_i.5, f32[2,75,32,128]{3,2,1,0:T(8,128)} %diff_j.5, s32[75,32,128]{2,1,0:T(8,128)S(1)} %copy-done.1), custom_call_target="tpu_custom_call" | custom-call | flops 100000000 | bytes 16000000 | tf_op jit(solution)/shard_map/pack_columns/pallas_call | solution.py:565
  14.4 0.0 collective-permute-done.75.recv_a
  14.4 0.0 collective-permute-done.76.recv_b
  14.4 3.0 %pack_ghost_columns.1 = (f32[3,160,128]{2,1,0:T(8,128)}, f32[3,160,128]{2,1,0:T(8,128)}) custom-call(f32[3,160,128]{2,1,0:T(8,128)} %get-tuple-element.543.columns_e, f32[3,160,128]{2,1,0:T(8,128)} %get-tuple-element.544.columns_o, f32[8,160,128]{2,1,0:T(8,128)} %collective-permute-done.75.recv_a, f32[8,160,128]{2,1,0:T(8,128)} %collective-permute-done.76.recv_b), custom_call_target="tpu_custom_call" | custom-call | tf_op jit(solution)/shard_map/pack_ghost_columns/pallas_call | solution.py:600
  17.4 1.6 %collective-permute-start.77 = (f32[3,160,128]{2,1,0:T(8,128)}, f32[3,160,128]{2,1,0:T(8,128)S(1)}, u32[]{:S(2)}, u32[]{:S(2)}) collective-permute-start(f32[3,160,128]{2,1,0:T(8,128)} %get-tuple-element.545), channel_id=1, source_target_pairs={{0,4},{4,0},{8,12},{12,8},{16,20},{20,16},{24,28},{28,24},{32,36},... | collective-permute-start | bytes 737288 | tf_op jit(solution)/shard_map/ppermute | solution.py:607
  19.1 6.3 %collective-permute-start.78 = (f32[3,160,128]{2,1,0:T(8,128)}, f32[3,160,128]{2,1,0:T(8,128)S(1)}, u32[]{:S(2)}, u32[]{:S(2)}) collective-permute-start(f32[3,160,128]{2,1,0:T(8,128)} %get-tuple-element.546), channel_id=1, source_target_pairs={{0,124},{4,8},{8,4},{12,16},{16,12},{20,24},{24,20},{28,32},{32,28... | collective-permute-start | bytes 737288 | tf_op jit(solution)/shard_map/ppermute | solution.py:608
  26.5 0.0 copy-start.4
  26.5 23.3 %conditional.7 = (f32[8,160,128]{2,1,0:T(8,128)}, f32[8,160,128]{2,1,0:T(8,128)}, f32[26,160,128]{2,1,0:T(8,128)}) conditional(s32[]{:T(128)} %clamp.3, (f32[8,160,128]{2,1,0:T(8,128)}, f32[2,75,32,128]{3,2,1,0:T(8,128)S(1)}, f32[2,75,32,128]{3,2,1,0:T(8,128)}, f32[2,75,32,128]{3,2,1,0:T(8,128)}, ...), branch_computations={%region_0.0_spmd, %region_1.2_spmd, %region_2.0_spmd, %region_3.0_... | conditional | flops 200000000 | bytes 21242984 | solution.py:625
  26.5 1.9 %collective-permute-start.2 = (f32[8,160,128]{2,1,0:T(8,128)}, f32[8,160,128]{2,1,0:T(8,128)}, u32[]{:S(2)}, u32[]{:S(2)}) collective-permute-start(f32[8,160,128]{2,1,0:T(8,128)} %get-tuple-element.365), channel_id=1, source_target_pairs={{3,7},{7,3},{11,127},{15,123},{19,119},{23,115},{27,111},{31,107},... | collective-permute-start | bytes 1966088 | tf_op jit(solution)/shard_map/cond/branch_1_fun/ppermute | solution.py:611
  28.5 6.5 %collective-permute-start.3 = (f32[8,160,128]{2,1,0:T(8,128)}, f32[8,160,128]{2,1,0:T(8,128)}, u32[]{:S(2)}, u32[]{:S(2)}) collective-permute-start(f32[8,160,128]{2,1,0:T(8,128)} %get-tuple-element.365), channel_id=1, source_target_pairs={{3,3},{7,127},{11,123},{15,119},{19,115},{23,111},{27,107},{31,103... | collective-permute-start | bytes 1966088 | tf_op jit(solution)/shard_map/cond/branch_1_fun/ppermute | solution.py:612
  35.0 14.3 %inner.33 = f32[26,160,128]{2,1,0:T(8,128)} custom-call(f32[2,75,32,128]{3,2,1,0:T(8,128)S(1)} %get-tuple-element.366.field, f32[2,75,32,128]{3,2,1,0:T(8,128)} %get-tuple-element.367.diff_i, f32[2,75,32,128]{3,2,1,0:T(8,128)} %get-tuple-element.368.diff_j, s32[75,32,128]{2,1,0:T(8,128)} %get-tuple-element.369.land), custom_call_target="tpu_custom_call" | custom-call | flops 200000000 | bytes 16000000 | tf_op jit(solution)/shard_map/cond/branch_1_fun/inner/pallas_call | solution.py:613
  49.3 0.0 collective-permute-done.2
  49.3 0.0 collective-permute-done.3
  49.8 0.0 copy-done.4
  49.8 0.0 collective-permute-done.77.recv_e
  49.8 0.0 copy-start.2
  49.8 0.0 collective-permute-done.78.recv_o
  49.8 0.0 copy-start.3
  49.9 0.7 %copy-done.2 = f32[3,160,128]{2,1,0:T(8,128)} copy-done((f32[3,160,128]{2,1,0:T(8,128)}, f32[3,160,128]{2,1,0:T(8,128)S(1)}, u32[]{:S(2)}) %copy-start.2) | copy-done | bytes 245784
  50.5 0.1 copy-done.3
  50.6 16.1 %finish.1 = f32[2,75,32,128]{3,2,1,0:T(8,128)} custom-call(f32[2,75,32,128]{3,2,1,0:T(8,128)S(1)} %copy-done, f32[2,75,32,128]{3,2,1,0:T(8,128)} %diff_i.5, f32[2,75,32,128]{3,2,1,0:T(8,128)} %diff_j.5, s32[75,32,128]{2,1,0:T(8,128)} %land.5, f32[26,160,128]{2,1,0:T(8,128)} %get-tuple-element.538.inner, f32[75,2,75]{2,1,0:T(2,128)} %bitcast.4, ...), custom_call_target="tpu_custom_call" | custom-call | tf_op jit(solution)/shard_map/finish/pallas_call | solution.py:628
  (1 shorter events, 0.0 us)
Async XLA Ops:
  0.0 5.4 %copy-start = (f32[2,75,32,128]{3,2,1,0:T(8,128)S(1)}, f32[2,75,32,128]{3,2,1,0:T(8,128)}, u32[]{:S(2)}) copy-start(f32[2,75,32,128]{3,2,1,0:T(8,128)} %field.5) | copy-start | bytes 7372804
  0.0 5.4 %copy-start.1 = (s32[75,32,128]{2,1,0:T(8,128)S(1)}, s32[75,32,128]{2,1,0:T(8,128)}, u32[]{:S(2)}) copy-start(s32[75,32,128]{2,1,0:T(8,128)} %land.5) | copy-start | bytes 3686404
  3.2 11.2 %collective-permute-start.75 = (f32[8,160,128]{2,1,0:T(8,128)}, f32[8,160,128]{2,1,0:T(8,128)}, u32[]{:S(2)}, u32[]{:S(2)}) collective-permute-start(f32[8,160,128]{2,1,0:T(8,128)} %get-tuple-element.540), channel_id=1, source_target_pairs={{0,1},{1,0},{2,3},{3,2},{4,5},{5,4},{6,7},{7,6},{8,9},{9,8},{10,11... | collective-permute-start | bytes 1966088 | tf_op jit(solution)/shard_map/ppermute | solution.py:598
  3.9 10.5 %collective-permute-start.76 = (f32[8,160,128]{2,1,0:T(8,128)}, f32[8,160,128]{2,1,0:T(8,128)}, u32[]{:S(2)}, u32[]{:S(2)}) collective-permute-start(f32[8,160,128]{2,1,0:T(8,128)} %get-tuple-element.537), channel_id=1, source_target_pairs={{1,2},{2,1},{5,6},{6,5},{9,10},{10,9},{13,14},{14,13},{17,18},{18,... | collective-permute-start | bytes 1966088 | tf_op jit(solution)/shard_map/ppermute | solution.py:599
  17.4 32.4 %collective-permute-start.77 = (f32[3,160,128]{2,1,0:T(8,128)}, f32[3,160,128]{2,1,0:T(8,128)S(1)}, u32[]{:S(2)}, u32[]{:S(2)}) collective-permute-start(f32[3,160,128]{2,1,0:T(8,128)} %get-tuple-element.545), channel_id=1, source_target_pairs={{0,4},{4,0},{8,12},{12,8},{16,20},{20,16},{24,28},{28,24},{32,36},... | collective-permute-start | bytes 737288 | tf_op jit(solution)/shard_map/ppermute | solution.py:607
  19.1 30.8 %collective-permute-start.78 = (f32[3,160,128]{2,1,0:T(8,128)}, f32[3,160,128]{2,1,0:T(8,128)S(1)}, u32[]{:S(2)}, u32[]{:S(2)}) collective-permute-start(f32[3,160,128]{2,1,0:T(8,128)} %get-tuple-element.546), channel_id=1, source_target_pairs={{0,124},{4,8},{8,4},{12,16},{16,12},{20,24},{24,20},{28,32},{32,28... | collective-permute-start | bytes 737288 | tf_op jit(solution)/shard_map/ppermute | solution.py:608
  26.5 23.3 %copy-start.4 = (s32[4096]{0:T(1024)S(1)}, s32[4096]{0:T(1024)}, u32[]{:S(2)}) copy-start(s32[4096]{0:T(1024)} %partner.3) | copy-start | bytes 49156
  26.5 22.8 %collective-permute-start.2 = (f32[8,160,128]{2,1,0:T(8,128)}, f32[8,160,128]{2,1,0:T(8,128)}, u32[]{:S(2)}, u32[]{:S(2)}) collective-permute-start(f32[8,160,128]{2,1,0:T(8,128)} %get-tuple-element.365), channel_id=1, source_target_pairs={{3,7},{7,3},{11,127},{15,123},{19,119},{23,115},{27,111},{31,107},... | collective-permute-start | bytes 1966088 | tf_op jit(solution)/shard_map/cond/branch_1_fun/ppermute | solution.py:611
  28.5 20.9 %collective-permute-start.3 = (f32[8,160,128]{2,1,0:T(8,128)}, f32[8,160,128]{2,1,0:T(8,128)}, u32[]{:S(2)}, u32[]{:S(2)}) collective-permute-start(f32[8,160,128]{2,1,0:T(8,128)} %get-tuple-element.365), channel_id=1, source_target_pairs={{3,3},{7,127},{11,123},{15,119},{19,115},{23,111},{27,107},{31,103... | collective-permute-start | bytes 1966088 | tf_op jit(solution)/shard_map/cond/branch_1_fun/ppermute | solution.py:612
  49.8 0.7 %copy-start.2 = (f32[3,160,128]{2,1,0:T(8,128)}, f32[3,160,128]{2,1,0:T(8,128)S(1)}, u32[]{:S(2)}) copy-start(f32[3,160,128]{2,1,0:T(8,128)S(1)} %collective-permute-done.77.recv_e) | copy-start | bytes 737284
  49.8 0.8 %copy-start.3 = (f32[3,160,128]{2,1,0:T(8,128)}, f32[3,160,128]{2,1,0:T(8,128)S(1)}, u32[]{:S(2)}) copy-start(f32[3,160,128]{2,1,0:T(8,128)S(1)} %collective-permute-done.78.recv_o) | copy-start | bytes 737284
